TPU v7x, 512 devices: a whole 4x4x16 slice. The times are simulated.
512 devices in a mesh: attn: 32 (over z, core), egrp: 4 (over x), eslice: 4 (over y).
Axes of the slice: x: 4, y: 4, z: 16, core: 2. Of those that a mesh axis runs over, the one named last changes fastest.
Arguments:
- queries: bfloat16 [384, 3072], P(('attn', 'eslice'), 'egrp'), may hold values from -20 to 20
- new_key: bfloat16 [384, 512], P(('attn', 'eslice'), 'egrp'), may hold values from -5 to 5
- new_value: bfloat16 [384, 512], P(('attn', 'eslice'), 'egrp'), may hold values from -5 to 5
- cache_keys: bfloat16 [384, 512, 512], P(('attn', 'eslice'), None, 'egrp'), may hold values from -20 to 20
- cache_values: bfloat16 [384, 512, 512], P(('attn', 'eslice'), None, 'egrp'), may hold values from -5 to 5
- lengths: int32 [384], P(('attn', 'eslice')), may hold values from 2 to 512, as said below
- out_proj: bfloat16 [4, 768, 6144], P('egrp', 'attn', 'eslice'), may hold values from -0.21875 to 0.21875
- residual: bfloat16 [384, 6144], P('attn', 'eslice'), may hold values from -24 to 24
- norm_gain: bfloat16 [6144], P('eslice'), may hold values from 0.25 to 1.75
- expert_ids: int32 [384, 4], P('attn'), may hold values from 0 to 7, all different within a row; in each aligned block of 384 rows (0 to 383, 384 to 767, ...) at most 288 rows name the same one
- gate_weights: bfloat16 [384, 4], P('attn'), may hold values from 0.099609375 to 1
- gate_proj: bfloat16 [8, 5376, 6144], P('egrp', 'attn', 'eslice'), may hold values from -0.078125 to 0.078125
- up_proj: bfloat16 [8, 5376, 6144], P('egrp', 'attn', 'eslice'), may hold values from -0.078125 to 0.078125
- down_proj: bfloat16 [8, 5376, 6144], P('egrp', 'attn', 'eslice'), may hold values from -0.15625 to 0.15625
Outputs:
- layer_out: bfloat16 [384, 6144], P(('attn', 'egrp'), 'eslice')
Inputs may be any that keep to these rules, and one draw needn't show every extreme that they name: `lengths`: some request has all 512 slots live. `expert_ids`: each request names 4 different experts; no expert is named by more than 288 requests, a bound that some block reaches.
All inputs are finite; a program needn't handle non-finite values.
Results may differ from a plain program's by a relative error of at most 0.02.
Values may be sent and summed in bfloat16 or wider, within the bound.
A program may use at most 64 MiB of HBM per device.

v0:
```python
import math

import jax
import jax.numpy as jnp
from jax import lax
from jax.sharding import PartitionSpec as P

D = 6144
HD = 128


eps = 1e-05


def attend_resident_cache(queries, new_key, new_value, cache_keys, cache_values, lengths):
    count = queries.shape[0]
    heads_kv = new_key.shape[1] // HD
    group = queries.shape[1] // (heads_kv * HD)
    span = cache_keys.shape[1]
    query_rows_full = queries.reshape(count, heads_kv, group, HD)
    k_old = cache_keys.reshape(count, span, heads_kv, HD)
    v_old = cache_values.reshape(count, span, heads_kv, HD)
    incoming_key = new_key.reshape(count, heads_kv, HD)
    v_new = new_value.reshape(count, heads_kv, HD).astype(jnp.float32)
    multiplier = 1.0 / math.sqrt(HD)
    scores = (
        jnp.einsum("bkgd,blkd->bkgl", query_rows_full, k_old, preferred_element_type=jnp.float32)
        * multiplier
    )
    self_score = (
        jnp.einsum(
            "zxlo,zxo->zxl", query_rows_full, incoming_key, preferred_element_type=jnp.float32
        )
        * multiplier
    )
    live = (jnp.arange(span)[None, :] < lengths[:, None])[:, None, None, :]
    scores = jnp.where(live, scores, -1e30)
    highest = jnp.maximum(jnp.max(scores, axis=-1), self_score)
    expos = jnp.where(live, jnp.exp(scores - highest[..., None]), 0.0)
    own_exp = jnp.exp(self_score - highest)
    totals = jnp.sum(expos, axis=-1) + own_exp
    weights = (expos / totals[..., None]).astype(jnp.bfloat16)
    own_weight = (own_exp / totals).astype(jnp.bfloat16)
    summed = jnp.einsum("bkgl,blkd->bkgd", weights, v_old, preferred_element_type=jnp.float32)
    summed = summed + own_weight.astype(jnp.float32)[..., None] * v_new[:, :, None, :]
    return summed.reshape(count, -1).astype(jnp.bfloat16)


def on_device(
    queries,
    new_key,
    new_value,
    cache_keys,
    cache_values,
    lengths,
    out_proj,
    residual,
    norm_gain,
    expert_ids,
    gate_weights,
    gate_proj,
    up_proj,
    down_proj,
):
    attended = attend_resident_cache(queries, new_key, new_value, cache_keys, cache_values, lengths)
    whole = lax.all_gather(attended, "eslice", axis=0, tiled=True)
    row_count = whole.shape[0]
    kv_local = out_proj.shape[0]
    wide = whole.reshape(row_count, kv_local, -1)
    width_local = out_proj.shape[2]
    partial_sum = jnp.einsum(
        "rkc,kcd->rd",
        wide,
        lax.all_gather(out_proj, "attn", axis=1, tiled=True),
        preferred_element_type=jnp.float32,
    )
    group_index = lax.axis_index("egrp")
    share_rows = row_count // lax.axis_size("egrp")
    mixed = lax.psum(partial_sum.astype(jnp.bfloat16), "egrp").astype(jnp.float32)
    hidden = (residual.astype(jnp.float32) + mixed).astype(jnp.bfloat16)
    hidden_f = hidden.astype(jnp.float32)
    first_sum, second_sum = lax.psum(
        (jnp.sum(hidden_f, axis=1), jnp.sum(hidden_f * hidden_f, axis=1)), "eslice"
    )
    center = first_sum / D
    spread = second_sum / D - center * center
    normed = (
        (hidden_f - center[:, None])
        * lax.rsqrt(spread + eps)[:, None]
        * norm_gain.astype(jnp.float32)[None, :]
    ).astype(jnp.bfloat16)
    tokens_full, routes_full, weights_full = (
        lax.all_gather(normed, "attn", axis=0, tiled=True),
        lax.all_gather(expert_ids, "attn", axis=0, tiled=True),
        lax.all_gather(gate_weights, "attn", axis=0, tiled=True),
    )
    total_rows = tokens_full.shape[0]
    capacity = total_rows * 3 // 4
    experts_local = gate_proj.shape[0]
    positions = jnp.arange(total_rows, dtype=jnp.int32)
    slot_range = jnp.arange(capacity, dtype=jnp.int32)
    slot_lists = []
    slot_scales = []
    for resident_expert in range(experts_local):
        expert_position = group_index * experts_local + resident_expert
        picked = routes_full == expert_position
        routed = jnp.any(picked, axis=1)
        weight_each = jnp.sum(jnp.where(picked, weights_full.astype(jnp.float32), 0.0), axis=1)
        order = jnp.cumsum(routed.astype(jnp.int32)) - 1
        target_slot = jnp.where(routed, order, capacity)
        slot_index = jnp.zeros((capacity,), jnp.int32).at[target_slot].set(positions, mode="drop")
        filled = jnp.sum(routed.astype(jnp.int32))
        scale_each = jnp.where(slot_range < filled, weight_each[slot_index], 0.0)
        slot_lists.append(slot_index)
        slot_scales.append(scale_each)
    slot_table = jnp.stack(slot_lists)
    scale_table = jnp.stack(slot_scales)
    collected_rows = tokens_full[slot_table]
    gate_part = jnp.einsum(
        "ecd,efd->ecf", collected_rows, gate_proj, preferred_element_type=jnp.float32
    )
    up_part = jnp.einsum(
        "ecd,efd->ecf", collected_rows, up_proj, preferred_element_type=jnp.float32
    )
    gate_total, up_total = (
        lax.psum(gate_part.astype(jnp.bfloat16), "eslice").astype(jnp.float32),
        lax.psum(up_part.astype(jnp.bfloat16), "eslice").astype(jnp.float32),
    )
    active = (jax.nn.silu(gate_total) * up_total).astype(jnp.bfloat16)
    produced = jnp.einsum("ecf,efd->ecd", active, down_proj, preferred_element_type=jnp.float32)
    weighted = produced * scale_table[:, :, None]
    term = (
        jnp.zeros((total_rows, width_local), jnp.float32)
        .at[slot_table.reshape(-1)]
        .add(weighted.reshape(-1, width_local))
    )
    moe = lax.psum_scatter(term, ("attn", "egrp"), scatter_dimension=0, tiled=True)
    hidden_own = lax.dynamic_slice_in_dim(hidden_f, group_index * share_rows, share_rows, 0)
    return (hidden_own + moe).astype(jnp.bfloat16)


def solution(mesh):
    placed = (
        P(("attn", "eslice"), "egrp"),
        P(("attn", "eslice"), "egrp"),
        P(("attn", "eslice"), "egrp"),
        P(("attn", "eslice"), None, "egrp"),
        P(("attn", "eslice"), None, "egrp"),
        P(("attn", "eslice")),
        P("egrp", "attn", "eslice"),
        P("attn", "eslice"),
        P("eslice"),
        P("attn", None),
        P("attn", None),
        P("egrp", "attn", "eslice"),
        P("egrp", "attn", "eslice"),
        P("egrp", "attn", "eslice"),
    )
    return jax.shard_map(
        on_device,
        mesh=mesh,
        in_specs=placed,
        out_specs=P(("attn", "egrp"), "eslice"),
        check_vma=False,
    )
```

profile of v0, /device:TPU:1, one launch (start us, length us, event | category | flops | bytes accessed | tf_op | source)
XLA Modules:
  0.0 626.8 jit_solution(1948595286494012093)
XLA Ops:
  6.5 0.7 all-gather.7.cloned.1.call-update
  7.3 0.7 reshape.347
  8.0 0.7 convert_element_type.89
  8.7 0.7 iota_compare_fusion
  9.4 0.8 fusion.30
  10.2 1.3 fusion.41
  11.5 0.2 fusion.19
  11.7 1.2 fusion.8
  13.0 10.4 %all-gather = bf16[4,3,768]{2,1,0:T(4,128)(2,1)S(1)} all-gather(bf16[1,3,768]{2,1,0:T(4,128)(2,1)S(1)} %reshape.406), channel_id=1, replica_groups=mesh['attn'=32,'egrp'=4,'eslice'=4] {'eslice'}, dimensions={0}, use_global_device_ids=true | all-gather | bytes 23040 | tf_op jit(solution)/shard_map/all_gather | solution.py:66
  23.4 0.7 convert_element_type.100
  24.1 39.9 %all-gather.3 = bf16[32,12,4]{1,2,0:T(4,128)(2,1)S(1)} all-gather(bf16[1,12,4]{1,2,0:T(4,128)(2,1)} %bitcast.59), channel_id=1, replica_groups=mesh['attn'=32,'egrp'=4,'eslice'=4] {'attn'}, dimensions={0}, use_global_device_ids=true | all-gather | bytes 3168 | tf_op jit(solution)/shard_map/all_gather | solution.py:95
  64.0 27.5 %all-gather.1 = s32[32,12,4]{1,2,0:T(4,128)S(1)} all-gather(s32[1,12,4]{1,2,0:T(4,128)} %bitcast.58), channel_id=1, replica_groups=mesh['attn'=32,'egrp'=4,'eslice'=4] {'attn'}, dimensions={0}, use_global_device_ids=true | all-gather | bytes 6336 | tf_op jit(solution)/shard_map/all_gather | solution.py:94
  91.5 2.1 fusion.2
  93.5 13.6 %psum.35 = bf16[12,1536]{1,0:T(8,128)(2,1)S(1)} all-reduce(bf16[12,1536]{1,0:T(8,128)(2,1)S(1)} %fusion.2), channel_id=1, replica_groups=mesh['attn'=32,'egrp'=4,'eslice'=4] {'egrp'}, use_global_device_ids=true, to_apply=%region_2.3 | all-reduce | flops 18432 | bytes 73728 | tf_op jit(solution)/shard_map/psum | solution.py:79
  107.2 0.1 convert_reduce_fusion
  107.3 8.2 %all-reduce.1 = (f32[12]{0:T(128)S(1)}, f32[12]{0:T(128)S(1)}) all-reduce(f32[12]{0:T(128)S(1)} %get-tuple-element.6, f32[12]{0:T(128)S(1)} %get-tuple-element.5), channel_id=1, replica_groups=mesh['attn'=32,'egrp'=4,'eslice'=4] {'eslice'}, use_global_device_ids=true, to_apply=%region_14.15 | all-reduce | flops 24 | bytes 192 | tf_op jit(solution)/shard_map/psum | solution.py:82
  115.6 0.7 fusion.18
  116.3 0.1 fusion.17
  116.6 0.1 reduce_or.23
  116.7 0.1 reduce_or.25
  116.9 0.1 reshape.353
  117.0 0.3 reduce-window.16
  117.4 0.1 reshape.354
  117.5 0.3 reduce-window.24
  117.9 0.1 slice_reduce_fusion.1
  118.1 2.9 scatter_custom_fusion
  121.1 0.1 slice_reduce_fusion
  121.3 2.9 scatter_custom_fusion.1
  124.4 0.1 reshape.428
  124.5 2.4 gather_fusion.1
  127.0 0.7 convert_reduce_fusion.2
  127.7 0.6 convert_reduce_fusion.1
  128.3 57.8 %all-gather.9.cloned.1.call-done = bf16[32,12,1536]{2,1,0:T(8,128)(2,1)} async-done(((bf16[1,12,1536]{2,1,0:T(8,128)(2,1)}), bf16[32,12,1536]{2,1,0:T(8,128)(2,1)}) %all-gather.9.cloned.1.call-update) | async-done | bytes 1179664 | tf_op jit(solution)/shard_map/all_gather | solution.py:93
  186.1 2.2 reshape.411
  188.4 3.6 gather_fusion
  192.0 3.2 convolution_convert_fusion
  195.1 1.6 convolution_convert_fusion.1
  196.7 0.2 all-reduce.6.cloned.1.call-start
  196.9 0.7 compare_select_fusion.5
  197.6 0.1 reshape.429
  197.8 2.4 gather_fusion.2
  200.3 0.7 compare_select_fusion.4
  201.0 48.8 %all-reduce.8.cloned.1.call-done = (bf16[2,288,168]{1,2,0:T(8,128)(2,1)}, bf16[2,288,168]{1,2,0:T(8,128)(2,1)}) async-done(((bf16[2,288,168]{1,2,0:T(8,128)(2,1)}, bf16[2,288,168]{1,2,0:T(8,128)(2,1)}), (bf16[2,288,168]{1,2,0:T(8,128)(2,1)}, bf16[2,288,168]{1,2,0:T(8,128)(2,1)})) %all-reduce.8.cloned.1.call-update) | async-done | bytes 387088 | tf_op jit(solution)/shard_map/psum | solution.py:127
  249.8 3.5 convolution_multiply_fusion
  253.4 13.2 %scatter_custom_fusion.2 = f32[384,1536]{1,0:T(8,128)} fusion(s32[576]{0:T(1024)S(1)} %fusion.26, f32[576,1536]{1,0:T(8,128)} %bitcast.55, f32[]{:T(128)} %constant.21.clone.1), kind=kCustom, calls=%fused_computation.12 | custom fusion | flops 884736 | bytes 2359808 | tf_op jit(solution)/shard_map/scatter-add | solution.py:135
  266.6 1.3 dynamic-slice
  268.5 350.2 %all-reduce.6.cloned.1.call-done = f32[384,1536]{1,0:T(8,128)} async-done(((f32[384,1536]{1,0:T(8,128)}), f32[384,1536]{1,0:T(8,128)}) %all-reduce.6.cloned.1.call-update) | async-done | bytes 2359312
  618.8 1.5 fusion.20
  (51 shorter events, 1.1 us)
Async XLA Ops:
  6.5 243.3 %copy-start = (bf16[2,168,1536]{2,1,0:T(8,128)(2,1)S(1)}, bf16[2,168,1536]{2,1,0:T(8,128)(2,1)}, u32[]{:S(2)}) copy-start(bf16[2,168,1536]{2,1,0:T(8,128)(2,1)} %param.27) | copy-start | bytes 3096580
  6.5 100.6 %copy-start.2 = (bf16[12,1536]{1,0:T(8,128)(2,1)S(1)}, bf16[12,1536]{1,0:T(8,128)(2,1)}, u32[]{:S(2)}) copy-start(bf16[12,1536]{1,0:T(8,128)(2,1)} %param.21) | copy-start | bytes 110596
  6.5 84.9 %all-gather.7.cloned.1.call-start = ((), (), s32[]{:S(2)}) async-start(), calls=%async_computation | async-start | bytes 2433024 | tf_op jit(solution)/shard_map/all_gather | solution.py:74
  7.3 178.9 %all-gather.9.cloned.1.call-start = ((), (), s32[]{:S(2)}) async-start(), calls=%async_computation.1 | async-start | bytes 1622016 | tf_op jit(solution)/shard_map/all_gather | solution.py:93
  116.3 133.5 %all-reduce.8.cloned.1.call-start = ((), (), s32[]{:S(2)}) async-start(), calls=%async_computation.3 | async-start | bytes 1032192 | tf_op jit(solution)/shard_map/psum | solution.py:127
  188.3 3.6 copy-start.3
  191.9 3.2 copy-start.1
  192.0 3.2 copy-start.4
  196.7 422.1 %all-reduce.6.cloned.1.call-start = ((), (), s32[]{:S(2)}) async-start(), calls=%async_computation.2 | async-start | bytes 4718592
Sparse Core Ops, SparseCore 0:
  9.5 78.0 all-gather.6
  116.4 69.6 all-gather.8
  196.8 52.9 all-reduce.7
  266.7 352.0 all-reduce.5
where the time goes:
time: 627 us
  waiting for transfers between devices  458 us (73%)
  blocking collectives  99.6 us (16%)
  other arithmetic  21.8 us (3%)
  local copies, waits for them, and re-layouts  19.8 us (3%)
  between operations  14 us (2%)
  matrix products  13.7 us (2%)
    unnamed x5, waiting for transfers between devices  351 us
    all_gather x1, waiting for transfers between devices, on_device(): lax.all_gather(normed, 'attn', axis=0, tiled=True)  57.8 us
    psum x1, waiting for transfers between devices, on_device(): lax.psum(up_part.astype(jnp.bfloat16), 'eslice').astype(jnp.float32)  48.8 us
    all_gather x1, blocking collectives, on_device(): lax.all_gather(gate_weights, 'attn', axis=0, tiled=True)  39.9 us
    all_gather x1, blocking collectives, on_device(): lax.all_gather(expert_ids, 'attn', axis=0, tiled=True)  27.5 us
    psum x1, blocking collectives, on_device(): lax.psum(partial_sum.astype(jnp.bfloat16), 'egrp').astype(jnp.float32)  13.6 us
    scatter-add x1, other arithmetic, on_device(): term = jnp.zeros((total_rows, width_local), jnp.float32).at[slot_table.re...  13.2 us
  transfers between devices with their start and end apart: 4, of which 3 were waited for; matrix products, arithmetic and copies ran while one was open for 4% of the time, Pallas kernels for 0%

commit v1 on v0

v1 whole, which is shorter than its diff:
```python
import functools
import math

import jax
import jax.numpy as jnp
from jax import lax
from jax.experimental import pallas as pl
from jax.experimental.pallas import tpu as pltpu
from jax.sharding import PartitionSpec as P

D = 6144
HD = 128
HG = 6
SPAN = 512
R = 3
EPS = 1e-05
NZ, NX = 16, 4
WD = D // NX
QW = WD // 4
KR = 24
KG = 768
F2 = 336
FC = 2 * F2
ZR = NZ * R
ROWS = NX * ZR
MESH = pl.DeviceIdType.MESH
BF = jnp.bfloat16
F32 = jnp.float32


def iota(shape, dim):
    return lax.broadcasted_iota(jnp.int32, shape, dim)


def onehot(cond):
    return jnp.where(cond, 1.0, 0.0).astype(BF)


def quotient(v, n):
    return (v * (65536 // n + 1)) >> 16


def mm(a, b):
    return jnp.dot(a, b, preferred_element_type=F32)


def mm_t(a, b):
    return lax.dot_general(a, b, (((1,), (1,)), ((), ())), preferred_element_type=F32)


def kernel(
    len_ref, q_ref, nk_ref, nv_ref, ck_ref, cv_ref, op_ref, res_ref, gain_ref, eid_ref, gw_ref,
    wg_ref, wu_ref, wd_ref,
    out_ref,
    wgu, wdn, w2, at, a2, xs, xr, st, hb, nm, gu, gr, ac, ms, mr, zs, zr,
    load_sem, wsend, wrecv, osend, orecv, csend, crecv, asend, arecv, xsend, xrecv, tsend, trecv,
    hsend, hrecv, fsend, frecv, gsend, grecv, bsend, brecv, msend, mrecv, zsend, zrecv,
):
    attn = lax.axis_index("attn")
    z, c = attn // 2, lax.rem(attn, 2)
    x, y = lax.axis_index("egrp"), lax.axis_index("eslice")

    def at_z(d):
        return (lax.rem(z + d + NZ, NZ) * 2 + c, x, y)

    def at_x(d):
        return (attn, lax.rem(x + d, NX), y)

    def at_y(d):
        return (attn, x, lax.rem(y + d, NX))

    sibling = (z * 2 + 1 - c, x, y)
    peers = [sibling]
    peers += [at_z(d) for d in range(1, NZ)]
    peers += [at_x(d) for d in range(1, NX)] + [at_y(d) for d in range(1, NX)]

    def send(src, dst, ssem, rsem, to):
        cp = pltpu.make_async_remote_copy(
            src_ref=src, dst_ref=dst, send_sem=ssem, recv_sem=rsem, device_id=to, device_id_type=MESH
        )
        cp.start()
        return cp

    def rows(ref, start, n):
        return ref.at[pl.ds(pl.multiple_of(start, 16), n)]

    barrier = pltpu.get_barrier_semaphore()
    for p in peers:
        pl.semaphore_signal(barrier, inc=1, device_id=p, device_id_type=MESH)

    loads = []
    for k, (src, dst, base) in enumerate(((wg_ref, wgu, 0), (wu_ref, wgu, FC), (wd_ref, wdn, 0))):
        cp = pltpu.make_async_copy(src, rows(dst, base + c * F2, F2), load_sem.at[k])
        cp.start()
        loads.append(cp)

    own = op_ref[...].astype(F32)
    block = jnp.concatenate([own[:, : WD // 2], own[:, WD // 2 :]], axis=0).astype(BF)
    w2[pl.ds(pl.multiple_of(attn * 2 * KR, 16), 2 * KR), :] = block

    with jax.named_scope("attention"):
        qf = q_ref[...].astype(F32)
        pad2 = jnp.zeros((2, HD), F32)
        pieces = []
        for r in range(R):
            pieces += [qf[r : r + 1, h * HD : (h + 1) * HD] for h in range(HG)] + [pad2]
        q24 = jnp.concatenate(pieces, axis=0)
        q32 = jnp.concatenate([q24, jnp.zeros((8, HD), F32)], axis=0).astype(BF)
        nk24 = jnp.concatenate([jnp.broadcast_to(nk_ref[r : r + 1, :].astype(F32), (8, HD)) for r in range(R)], 0)
        nv24 = jnp.concatenate([jnp.broadcast_to(nv_ref[r : r + 1, :].astype(F32), (8, HD)) for r in range(R)], 0)
        len24 = jnp.concatenate([jnp.full((8, 1), len_ref[r], jnp.int32) for r in range(R)], 0)
        scale = 1.0 / math.sqrt(HD)
        scores = jnp.concatenate([mm_t(q32, ck_ref[r])[r * 8 : (r + 1) * 8] for r in range(R)], 0) * scale
        self_score = jnp.sum(q24 * nk24, axis=1, keepdims=True) * scale
        live = iota((R * 8, SPAN), 1) < len24
        scores = jnp.where(live, scores, -1e30)
        highest = jnp.maximum(jnp.max(scores, axis=1, keepdims=True), self_score)
        expos = jnp.where(live, jnp.exp(scores - highest), 0.0)
        own_exp = jnp.exp(self_score - highest)
        totals = jnp.sum(expos, axis=1, keepdims=True) + own_exp
        weights = jnp.concatenate([expos / totals, jnp.zeros((8, SPAN), F32)], axis=0).astype(BF)
        own_weight = (own_exp / totals).astype(BF).astype(F32)
        summed = jnp.concatenate([mm(weights, cv_ref[r])[r * 8 : (r + 1) * 8] for r in range(R)], 0)
        summed = summed + own_weight * nv24
        at[pl.ds(pl.multiple_of(y * 32, 16), 32), :] = jnp.concatenate(
            [summed, jnp.zeros((8, HD), F32)], axis=0
        ).astype(BF)

    with jax.named_scope("entry"):
        pl.semaphore_wait(barrier, len(peers))

    sends = []
    a_cps = []
    mine = rows(at, y * 32, 32)
    for d in range(1, NX):
        a_cps.append(send(mine, mine, asend.at[d - 1], arecv.at[d - 1], at_y(d)))
    o_cps = {}
    c_cps = []

    def block_of(d):
        return rows(w2, (lax.rem(z - d + 2 * NZ, NZ) * 2 + c) * 2 * KR, 2 * KR)

    def pass_on(d, sign):
        for s in (2, 1):
            far = d + s
            if far > (NZ // 2 if sign > 0 else NZ // 2 - 1):
                continue
            k = far - 1 if sign > 0 else NZ // 2 + far - 1
            o_cps[sign * far] = send(
                block_of(sign * d), block_of(sign * d), osend.at[k], orecv.at[k], at_z(sign * s)
            )

    def to_sibling(d):
        k = d + NZ // 2 - 1
        c_cps.append(send(block_of(d), block_of(d), csend.at[k], crecv.at[k], sibling))

    pass_on(0, 1)
    pass_on(0, -1)
    to_sibling(0)
    w_cps = []
    for k, (src, dst, base) in enumerate(((wg_ref, wgu, 0), (wu_ref, wgu, FC), (wd_ref, wdn, 0))):
        w_cps.append(send(src, rows(dst, base + c * F2, F2), wsend.at[k], wrecv.at[k], sibling))

    row16, lane16 = iota((16, 4 * R), 0), iota((16, 4 * R), 1)
    part = row16 & 3
    wanted = (lane16 == x * R + part) & (part < R)
    res16 = jnp.zeros((16, QW), F32)
    for q in range(4):
        res16 = res16 + mm(onehot(wanted & ((row16 >> 2) == q)), res_ref[:, q * QW : (q + 1) * QW])
    gain16 = jnp.concatenate(
        [jnp.broadcast_to(gain_ref[:, q * QW : (q + 1) * QW].astype(F32), (4, QW)) for q in range(4)], 0
    )
    first = (iota((4 * R, 128), 0) - x * R) * 8
    share_row = jnp.zeros((1, 128), F32)
    lane12 = iota((4 * R, 128), 1)
    gwf = gw_ref[...].astype(F32)
    for k in range(4):
        hit = (lane12 == first + eid_ref[:, k : k + 1]) & (first >= 0) & (first < 8 * R)
        share_row = share_row + jnp.sum(jnp.where(hit, gwf[:, k : k + 1], 0.0), axis=0, keepdims=True)

    with jax.named_scope("attended_gather"):
        for cp in a_cps:
            cp.wait_recv()
        p, s = iota((HG * 16, 128), 0), iota((HG * 16, 128), 1)
        pick = onehot(s == ((p >> 2) & 3) * 32 + (p & 3) * 8 + (p >> 4))
        heads = mm(pick, at[...]).astype(BF)
        a16 = jnp.concatenate([heads[h * 16 : (h + 1) * 16] for h in range(HG)], axis=1)
        j = iota((1, 2 * KG), 1)
        blk = quotient(j, 2 * KR)
        rem = j - blk * 2 * KR
        second = rem >= KR
        source = blk * KR + jnp.where(second, rem - KR, rem)
        n = 512
        for t in range(2 * KG // n):
            cols = slice(t * n, (t + 1) * n)
            spread_out = mm(a16, onehot(iota((KG, n), 0) == source[:, cols]))
            later = second[:, cols]
            a2[:, cols] = jnp.concatenate(
                [jnp.where(later, 0.0, spread_out), jnp.where(later, spread_out, 0.0)], axis=0
            ).astype(BF)

    with jax.named_scope("projection_gather"):
        for d in range(1, NZ // 2 + 1):
            for sign in (1, -1):
                if sign * d not in o_cps:
                    continue
                o_cps[sign * d].wait_recv()
                if d % 2 == 0:
                    pass_on(d, sign)
                to_sibling(sign * d)
        for cp in c_cps:
            cp.wait_recv()

    with jax.named_scope("projection"):
        mixed = jnp.zeros((32, WD // 2), F32)
        for t in range(4):
            n = 2 * KG // 4
            mixed = mixed + mm(a2[:, t * n : (t + 1) * n], w2[t * n : (t + 1) * n, :])
        mixed = mixed.astype(BF)
        p, s = iota((64, 32), 0), iota((64, 32), 1)
        source = (((p >> 3) & 1) << 4) + ((p >> 4) << 2) + (p & 3)
        odd = ((p >> 2) & 1) == 1
        xs[...] = (
            mm(onehot((s == source) & ~odd), mixed[:, :QW]) + mm(onehot((s == source) & odd), mixed[:, QW:])
        ).astype(BF)

    with jax.named_scope("projection_terms"):
        cps = []
        for d in range(1, NX):
            to = lax.rem(x + d, NX)
            cps.append(send(rows(xs, to * 16, 16), rows(xr, x * 16, 16), xsend.at[d - 1], xrecv.at[d - 1], at_x(d)))
        for cp in cps:
            cp.wait_recv()
        sends += cps
        xr[pl.ds(pl.multiple_of(x * 16, 16), 16), :] = xs[pl.ds(pl.multiple_of(x * 16, 16), 16), :]
        terms = xr[...].astype(F32)
        hidden = res16 + ((terms[0:16] + terms[16:32]) + (terms[32:48] + terms[48:64]))
        hidden = hidden.astype(BF).astype(F32)

    with jax.named_scope("layer_norm"):
        lane = iota((16, 128), 1)
        s1 = jnp.sum(hidden, axis=1, keepdims=True)
        s2 = jnp.sum(hidden * hidden, axis=1, keepdims=True)
        mine = rows(st, y * 16, 16)
        st[pl.ds(pl.multiple_of(y * 16, 16), 16), :] = jnp.where(lane == 0, s1, jnp.where(lane == 1, s2, 0.0))
        cps = [send(mine, mine, tsend.at[d - 1], trecv.at[d - 1], at_y(d)) for d in range(1, NX)]
        for cp in cps:
            cp.wait_recv()
        sends += cps
        stats = st[...]
        stats = (stats[0:16] + stats[16:32]) + (stats[32:48] + stats[48:64])
        stats = stats[0:8] + stats[8:16]
        stats = stats[0:4] + stats[4:8]
        stats = jnp.concatenate([stats] * 4, axis=0)
        center = stats[:, 0:1] / D
        spread = stats[:, 1:2] / D - center * center
        normed = (hidden - center) * lax.rsqrt(spread + EPS) * gain16
        pad = (iota((16, QW), 0) & 3) == 3
        extra = jnp.concatenate([share_row, jnp.zeros((1, QW - 128), F32)], axis=1)
        extra = jnp.where(iota((16, QW), 0) == 3, extra, 0.0)
        hb[pl.ds(pl.multiple_of((x * NZ + z) * 16, 16), 16), :] = jnp.where(pad, extra, normed).astype(BF)

    with jax.named_scope("token_gather"):
        f_cps = []

        def over_x(d):
            blk = rows(hb, (x * NZ + lax.rem(z - d + NZ, NZ)) * 16, 16)
            for k in range(1, NX):
                n = (k - 1) * NZ + d
                f_cps.append(send(blk, blk, fsend.at[n], frecv.at[n], at_x(k)))

        blk = rows(hb, (x * NZ + z) * 16, 16)
        order = [8] + [v for i in range(7, 0, -1) for v in (i, NZ - i)]
        h_cps = {d: send(blk, blk, hsend.at[d], hrecv.at[d], at_z(d)) for d in order}
        over_x(0)
        for d in sorted(order, key=lambda v: min(v, NZ - v)):
            h_cps[d].wait_recv()
            over_x(d)
        for cp in f_cps:
            cp.wait_recv()

    with jax.named_scope("compact"):
        p, s = iota((4 * ZR, NZ * 16), 0), iota((4 * ZR, NZ * 16), 1)
        quarter = quotient(p, ZR)
        m = p - quarter * ZR
        who = quotient(m, R)
        pick = onehot(s == who * 16 + quarter * 4 + (m - who * R))
        for g in range(NX):
            got = mm(pick, hb[g * NZ * 16 : (g + 1) * NZ * 16, :]).astype(BF)
            for q in range(4):
                nm[g * ZR : (g + 1) * ZR, q * QW : (q + 1) * QW] = got[q * ZR : (q + 1) * ZR]
        p, s = iota((ZR, NZ * 16), 0), iota((ZR, NZ * 16), 1)
        who = quotient(p, R)
        shares = mm(onehot(s == who * 16 + 3), hb[pl.ds(pl.multiple_of(y * NZ * 16, 16), NZ * 16), 0:128])
        lane = iota((ZR, 128), 1)
        place = (iota((ZR, 128), 0) - quotient(iota((ZR, 128), 0), R) * R) * 8 + x * 2
        share0 = jnp.sum(jnp.where(lane == place, shares, 0.0), axis=1, keepdims=True)
        share1 = jnp.sum(jnp.where(lane == place + 1, shares, 0.0), axis=1, keepdims=True)

    with jax.named_scope("gate_up"):
        for cp in loads:
            cp.wait()
        for cp in w_cps:
            cp.wait_recv()
        tokens = nm[...]
        for lo, hi in ((0, 512), (512, 1024), (1024, 2 * FC)):
            gu[:, lo:hi] = mm_t(tokens, wgu[lo:hi, :]).astype(BF)

    with jax.named_scope("gate_up_terms"):
        cps = []
        for d in range(1, NX):
            to = lax.rem(y + d, NX)
            cps.append(send(rows(gu, to * ZR, ZR), rows(gr, y * ZR, ZR), gsend.at[d - 1], grecv.at[d - 1], at_y(d)))
        for cp in cps:
            cp.wait_recv()
        sends += cps
        gr[pl.ds(pl.multiple_of(y * ZR, 16), ZR), :] = gu[pl.ds(pl.multiple_of(y * ZR, 16), ZR), :]

    with jax.named_scope("activation"):
        total = gr[0:ZR, :].astype(F32)
        for g in range(1, NX):
            total = total + gr[g * ZR : (g + 1) * ZR, :].astype(F32)
        gate, up = total[:, :FC], total[:, FC:]
        unit = iota((ZR, FC), 1)
        unit = jnp.where(unit >= F2, unit - F2, unit)
        share = jnp.where(unit >= F2 // 2, share1, share0)
        mine = rows(ac, y * ZR, ZR)
        ac[pl.ds(pl.multiple_of(y * ZR, 16), ZR), :] = (gate / (1.0 + jnp.exp(-gate)) * up * share).astype(BF)

    with jax.named_scope("activation_gather"):
        cps = [send(mine, mine, bsend.at[d - 1], brecv.at[d - 1], at_y(d)) for d in range(1, NX)]
        for cp in cps:
            cp.wait_recv()
        sends += cps

    with jax.named_scope("down"):
        act = ac[...]
        for t in range(3):
            n = WD // 3
            ms[:, t * n : (t + 1) * n] = mm(act, wdn[:, t * n : (t + 1) * n]).astype(BF)

    with jax.named_scope("expert_sum_x"):
        cps = []
        for d in range(1, NX):
            to = lax.rem(x + d, NX)
            cps.append(send(rows(ms, to * ZR, ZR), rows(mr, x * ZR, ZR), msend.at[d - 1], mrecv.at[d - 1], at_x(d)))
        for cp in cps:
            cp.wait_recv()
        sends += cps
        mr[pl.ds(pl.multiple_of(x * ZR, 16), ZR), :] = ms[pl.ds(pl.multiple_of(x * ZR, 16), ZR), :]
        total = mr[0:ZR, :].astype(F32)
        for g in range(1, NX):
            total = total + mr[g * ZR : (g + 1) * ZR, :].astype(F32)
        total = total.astype(BF)
        p, s = iota((NZ * 16, ZR), 0), iota((NZ * 16, ZR), 1)
        wanted = (s == (p >> 4) * R + (p & 3)) & ((p & 3) < R)
        piece = jnp.zeros((NZ * 16, QW), F32)
        for q in range(4):
            piece = piece + mm(onehot(wanted & (((p >> 2) & 3) == q)), total[:, q * QW : (q + 1) * QW])
        zs[...] = piece.astype(BF)

    with jax.named_scope("expert_sum_z"):
        cps = []
        for d in order:
            to = lax.rem(z + d, NZ)
            cps.append(send(rows(zs, to * 16, 16), rows(zr, z * 16, 16), zsend.at[d], zrecv.at[d], at_z(d)))
        for cp in cps:
            cp.wait_recv()
        sends += cps
        zr[pl.ds(pl.multiple_of(z * 16, 16), 16), :] = zs[pl.ds(pl.multiple_of(z * 16, 16), 16), :]
        total = hidden
        for g in range(NZ):
            total = total + zr[g * 16 : (g + 1) * 16, :].astype(F32)
        for q in range(4):
            out_ref[:, q * QW : (q + 1) * QW] = total[q * 4 : q * 4 + R, :].astype(BF)

    with jax.named_scope("drain"):
        for cp in a_cps + list(o_cps.values()) + c_cps + w_cps + list(h_cps.values()) + f_cps + sends:
            cp.wait_send()


def on_device(
    queries, new_key, new_value, cache_keys, cache_values, lengths, out_proj, residual, norm_gain,
    expert_ids, gate_weights, gate_proj, up_proj, down_proj,
):
    vmem = pl.BlockSpec(memory_space=pltpu.VMEM)
    dma = pltpu.SemaphoreType.DMA
    return pl.pallas_call(
        kernel,
        out_shape=jax.ShapeDtypeStruct((R, WD), BF),
        in_specs=[pl.BlockSpec(memory_space=pltpu.SMEM)] + [vmem] * 10 + [pl.BlockSpec(memory_space=pl.ANY)] * 3,
        out_specs=vmem,
        scratch_shapes=[
            pltpu.VMEM((2 * FC, WD), BF),
            pltpu.VMEM((FC, WD), BF),
            pltpu.VMEM((2 * KG, WD // 2), BF),
            pltpu.VMEM((NX * 32, HD), BF),
            pltpu.VMEM((32, 2 * KG), BF),
            pltpu.VMEM((64, QW), BF),
            pltpu.VMEM((64, QW), BF),
            pltpu.VMEM((64, 128), F32),
            pltpu.VMEM((NX * NZ * 16, QW), BF),
            pltpu.VMEM((ROWS, WD), BF),
            pltpu.VMEM((ROWS, 2 * FC), BF),
            pltpu.VMEM((ROWS, 2 * FC), BF),
            pltpu.VMEM((ROWS, FC), BF),
            pltpu.VMEM((ROWS, WD), BF),
            pltpu.VMEM((ROWS, WD), BF),
            pltpu.VMEM((NZ * 16, QW), BF),
            pltpu.VMEM((NZ * 16, QW), BF),
            dma((3,)),
            dma((3,)), dma((3,)),
            dma((NZ,)), dma((NZ,)),
            dma((NZ,)), dma((NZ,)),
            dma((3,)), dma((3,)),
            dma((3,)), dma((3,)),
            dma((3,)), dma((3,)),
            dma((NZ,)), dma((NZ,)),
            dma((3 * NZ,)), dma((3 * NZ,)),
            dma((3,)), dma((3,)),
            dma((3,)), dma((3,)),
            dma((3,)), dma((3,)),
            dma((NZ,)), dma((NZ,)),
        ],
        compiler_params=pltpu.CompilerParams(
            collective_id=0, has_side_effects=True, vmem_limit_bytes=48 << 20
        ),
        name="decode_layer",
    )(
        lengths, queries, new_key, new_value, cache_keys, cache_values,
        out_proj.reshape(KR, WD), residual, norm_gain.reshape(1, WD), expert_ids, gate_weights,
        gate_proj.reshape(F2, WD), up_proj.reshape(F2, WD), down_proj.reshape(F2, WD),
    )


def solution(mesh):
    placed = (
        P(("attn", "eslice"), "egrp"),
        P(("attn", "eslice"), "egrp"),
        P(("attn", "eslice"), "egrp"),
        P(("attn", "eslice"), None, "egrp"),
        P(("attn", "eslice"), None, "egrp"),
        P(("attn", "eslice")),
        P("egrp", "attn", "eslice"),
        P("attn", "eslice"),
        P("eslice"),
        P("attn", None),
        P("attn", None),
        P("egrp", "attn", "eslice"),
        P("egrp", "attn", "eslice"),
        P("egrp", "attn", "eslice"),
    )
    return jax.shard_map(
        on_device, mesh=mesh, in_specs=placed, out_specs=P(("attn", "egrp"), "eslice"), check_vma=False
    )
```

time: 627 us -> 121 us (0.19)
  waiting for transfers between devices: 458 us -> 0 us
  Pallas kernels: 0 us -> 111 us
  blocking collectives: 99.6 us -> 0 us
  other arithmetic: 21.8 us -> 0 us
  between operations: 14 us -> 0.04 us
  matrix products: 13.7 us -> 0 us
  local copies, waits for them, and re-layouts: 19.8 us -> 10.1 us
    unnamed x5 -> x0, waiting for transfers between devices: 351 us -> none
    pallas_call x0 -> x1, Pallas kernels: none -> 111 us  [on_device(): pl.pallas_call(kernel, out_shape=jax.ShapeDtypeStruct((R, WD), BF), in_sp...]
    all_gather x3 -> x0, blocking collectives: 77.8 us -> none  [the longest x1 39.9 us: on_device(): lax.all_gather(gate_weights, 'attn', axis=0, tiled=True)]
    all_gather x2 -> x0, waiting for transfers between devices: 57.8 us -> none  [the longest x1 57.8 us: on_device(): lax.all_gather(normed, 'attn', axis=0, tiled=True)]
    psum x1 -> x0, waiting for transfers between devices: 48.8 us -> none  [on_device(): lax.psum(up_part.astype(jnp.bfloat16), 'eslice').astype(jnp.float32)]
    psum x2 -> x0, blocking collectives: 21.8 us -> none  [the longest x1 13.6 us: on_device(): lax.psum(partial_sum.astype(jnp.bfloat16), 'egrp').astype(jnp.float32)]
    dot_general x7 -> x0, matrix products: 13.7 us -> none  [the longest x1 3.55 us: on_device(): jnp.einsum('ecf,efd->ecd', active, down_proj, preferred_element_type=jnp....]
    scatter-add x1 -> x0, other arithmetic: 13.2 us -> none  [on_device(): term = jnp.zeros((total_rows, width_local), jnp.float32).at[slot_table.re...]
  transfers between devices with their start and end apart: 4 -> 0, of which waited for: 3 -> 0; matrix products, arithmetic and copies ran while one was open for 4% -> 0% of each run, Pallas kernels for 0% -> 0%
where the time goes in v1:
time: 121 us
  Pallas kernels  111 us (92%)
  local copies, waits for them, and re-layouts  10.1 us (8%)
    pallas_call x1, Pallas kernels, on_device(): pl.pallas_call(kernel, out_shape=jax.ShapeDtypeStruct((R, WD), BF), in_sp...  111 us
    unnamed x31, local copies, waits for them, and re-layouts  10.1 us

profile of v1, /device:TPU:1, one launch (start us, length us, event | category | flops | bytes accessed | tf_op | source)
XLA Modules:
  0.0 120.9 jit_solution(5095642529577303483)
XLA Ops:
  0.0 0.0 copy-start.13
  0.0 0.0 copy-start.11
  0.0 0.7 copy-done.13
  0.7 0.1 copy.16.gw_ref
  0.8 0.0 copy-done.11
  0.8 0.0 copy-start.12
  0.8 0.7 copy-done.12
  1.5 0.0 copy-start.7
  1.5 0.0 copy-start.8
  1.5 0.0 copy-start.9
  1.5 0.0 copy-start.10
  1.5 0.1 copy.15.eid_ref
  1.6 0.6 copy-done.7
  2.2 0.0 copy-done.8
  2.2 0.0 copy-done.9
  2.2 0.0 copy-done.10
  2.2 0.0 copy-start
  2.2 1.2 %copy-done = bf16[2,168,1536]{2,1,0:T(8,128)(2,1)S(1)} copy-done((bf16[2,168,1536]{2,1,0:T(8,128)(2,1)S(1)}, bf16[2,168,1536]{2,1,0:T(8,128)(2,1)}, u32[]{:S(2)}) %copy-start) | copy-done | bytes 1032216
  3.4 0.0 copy-start.1
  3.4 1.2 %copy-done.1 = bf16[2,168,1536]{2,1,0:T(8,128)(2,1)S(1)} copy-done((bf16[2,168,1536]{2,1,0:T(8,128)(2,1)S(1)}, bf16[2,168,1536]{2,1,0:T(8,128)(2,1)}, u32[]{:S(2)}) %copy-start.1) | copy-done | bytes 1032216
  4.6 0.0 copy-start.2
  4.6 1.2 %copy-done.2 = bf16[2,168,1536]{2,1,0:T(8,128)(2,1)S(1)} copy-done((bf16[2,168,1536]{2,1,0:T(8,128)(2,1)S(1)}, bf16[2,168,1536]{2,1,0:T(8,128)(2,1)}, u32[]{:S(2)}) %copy-start.2) | copy-done | bytes 1032216
  5.8 0.0 copy-start.3
  5.8 1.0 copy-done.3
  6.8 0.0 copy-start.4
  6.8 1.0 copy-done.4
  7.8 0.0 copy-start.5
  7.8 0.9 copy-done.5
  8.7 0.0 copy-start.6
  8.7 0.8 copy-done.6
  9.5 110.8 %decode_layer.1 = bf16[3,1536]{1,0:T(4,128)(2,1)S(1)} custom-call(s32[3]{0:T(128)S(1)} %copy-done.10, bf16[3,768]{1,0:T(4,128)(2,1)S(1)} %copy-done.7, bf16[3,128]{1,0:T(4,128)(2,1)S(1)} %copy-done.8, bf16[3,128]{1,0:T(4,128)(2,1)S(1)} %copy-done.9, bf16[3,512,128]{2,1,0:T(8,128)(2,1)S(1)} %copy-done.3, bf16[3,512,128]{2,1,0:T(8,128)(2,1)S(1)} %copy-done.4, ...), custom_call_target="tpu_custom_call" | custom-call | tf_op jit(solution)/shard_map/decode_layer/pallas_call | solution.py:388
  120.3 0.6 copy.18
  (1 shorter events, 0.0 us)
Async XLA Ops:
  0.0 0.7 copy-start.13
  0.0 0.8 copy-start.11
  0.8 0.7 copy-start.12
  1.5 0.7 copy-start.7
  1.5 0.7 copy-start.8
  1.5 0.7 copy-start.9
  1.5 0.7 copy-start.10
  2.2 1.2 %copy-start = (bf16[2,168,1536]{2,1,0:T(8,128)(2,1)S(1)}, bf16[2,168,1536]{2,1,0:T(8,128)(2,1)}, u32[]{:S(2)}) copy-start(bf16[2,168,1536]{2,1,0:T(8,128)(2,1)} %param.25) | copy-start | bytes 3096580
  3.4 1.2 %copy-start.1 = (bf16[2,168,1536]{2,1,0:T(8,128)(2,1)S(1)}, bf16[2,168,1536]{2,1,0:T(8,128)(2,1)}, u32[]{:S(2)}) copy-start(bf16[2,168,1536]{2,1,0:T(8,128)(2,1)} %param.26) | copy-start | bytes 3096580
  4.6 1.2 %copy-start.2 = (bf16[2,168,1536]{2,1,0:T(8,128)(2,1)S(1)}, bf16[2,168,1536]{2,1,0:T(8,128)(2,1)}, u32[]{:S(2)}) copy-start(bf16[2,168,1536]{2,1,0:T(8,128)(2,1)} %param.27) | copy-start | bytes 3096580
  5.8 1.0 copy-start.3
  6.8 1.0 copy-start.4
  7.8 0.9 copy-start.5
  8.7 0.8 copy-start.6

commit v2 on v1

v2 whole, which is shorter than its diff:
```python
import functools
import math

import jax
import jax.numpy as jnp
from jax import lax
from jax.experimental import pallas as pl
from jax.experimental.pallas import tpu as pltpu
from jax.sharding import PartitionSpec as P

D = 6144
HD = 128
HG = 6
SPAN = 512
R = 3
EPS = 1e-05
NZ, NX = 16, 4
WD = D // NX
QW = WD // 4
KR = 24
KG = 768
F2 = 336
FC = 2 * F2
ZR = NZ * R
GW = 2 * FC + 64
ROWS = NX * ZR
MESH = pl.DeviceIdType.MESH
BF = jnp.bfloat16
F32 = jnp.float32


def iota(shape, dim):
    return lax.broadcasted_iota(jnp.int32, shape, dim)


def onehot(cond):
    return jnp.where(cond, 1.0, 0.0).astype(BF)


def quotient(v, n):
    return (v * (65536 // n + 1)) >> 16


def mm(a, b):
    return jnp.dot(a, b, preferred_element_type=F32)


def mm_t(a, b):
    return lax.dot_general(a, b, (((1,), (1,)), ((), ())), preferred_element_type=F32)


def kernel(
    len_ref, q_hbm, nk_hbm, nv_hbm, ck_hbm, cv_hbm, op_hbm, res_hbm, gain_hbm, eid_hbm, gw_hbm,
    wg_ref, wu_ref, wd_ref,
    out_ref,
    qv, nkv, nvv, ckv, cvv, opv, resv, gainv, eidv, gwv, wgu, wdn, w2, at, a2, xs, xr, gs, hb, nm, gu, gr, ac, ms, mr, zs, zr,
    load_sem, wsend, wrecv, osend, orecv, csend, crecv, asend, arecv, xsend, xrecv, tsend, trecv,
    hsend, hrecv, fsend, frecv, gsend, grecv, bsend, brecv, msend, mrecv, zsend, zrecv,
):
    attn = lax.axis_index("attn")
    z, c = attn // 2, lax.rem(attn, 2)
    x, y = lax.axis_index("egrp"), lax.axis_index("eslice")

    def at_z(d):
        return (lax.rem(z + d + NZ, NZ) * 2 + c, x, y)

    def at_x(d):
        return (attn, lax.rem(x + d, NX), y)

    def at_y(d):
        return (attn, x, lax.rem(y + d, NX))

    quad, seat = z // 4, lax.rem(z, 4)

    def in_quad(s, dx, dy):
        return ((quad * 4 + s) * 2 + c, lax.rem(x + dx, NX), lax.rem(y + dy, NX))

    sibling = (z * 2 + 1 - c, x, y)
    others = [(k // 4, k % 4) for k in range(1, 16)]
    peers = [sibling]
    peers += [at_z(d) for d in range(1, NZ)]
    peers += [at_x(d) for d in range(1, NX)] + [at_y(d) for d in range(1, NX)]
    peers += [in_quad(lax.rem(seat + k, 4), m, 0) for k, m in others if k and m]
    peers += [in_quad(lax.rem(seat + k, 4), 0, m) for k, m in others if k and m]

    def send(src, dst, ssem, rsem, to):
        cp = pltpu.make_async_remote_copy(
            src_ref=src, dst_ref=dst, send_sem=ssem, recv_sem=rsem, device_id=to, device_id_type=MESH
        )
        cp.start()
        return cp

    def rows(ref, start, n):
        return ref.at[pl.ds(pl.multiple_of(start, 16), n)]

    barrier = pltpu.get_barrier_semaphore()
    for p in peers:
        pl.semaphore_signal(barrier, inc=1, device_id=p, device_id_type=MESH)

    def load(src, dst, sem):
        cp = pltpu.make_async_copy(src, dst, sem)
        cp.start()
        return cp

    l_q, l_nk, l_nv, l_ck, l_cv, l_op = [
        load(src, dst, load_sem.at[k])
        for k, (src, dst) in enumerate(
            ((q_hbm, qv), (nk_hbm, nkv), (nv_hbm, nvv), (ck_hbm, ckv), (cv_hbm, cvv), (op_hbm, opv))
        )
    ]
    l_rest = [
        load(src, dst, load_sem.at[k + 6])
        for k, (src, dst) in enumerate(((res_hbm, resv), (gain_hbm, gainv), (eid_hbm, eidv), (gw_hbm, gwv)))
    ]
    expert_weights = ((wg_ref, wgu, 0), (wu_ref, wgu, FC), (wd_ref, wdn, 0))
    loads = [
        load(src, rows(dst, base + c * F2, F2), load_sem.at[k + 10])
        for k, (src, dst, base) in enumerate(expert_weights)
    ]

    l_op.wait()
    own = opv[...].astype(F32)
    block = jnp.concatenate([own[:, : WD // 2], own[:, WD // 2 :]], axis=0).astype(BF)
    w2[pl.ds(pl.multiple_of((quad * 2 + c) * 2 * KR, 16), 2 * KR), :] = block

    with jax.named_scope("attention"):
        for cp in (l_q, l_nk, l_nv, l_ck, l_cv):
            cp.wait()
        qf = qv[...].astype(F32)
        pad2 = jnp.zeros((2, HD), F32)
        pieces = []
        for r in range(R):
            pieces += [qf[r : r + 1, h * HD : (h + 1) * HD] for h in range(HG)] + [pad2]
        q24 = jnp.concatenate(pieces, axis=0)
        q32 = jnp.concatenate([q24, jnp.zeros((8, HD), F32)], axis=0).astype(BF)
        nk24 = jnp.concatenate([jnp.broadcast_to(nkv[r : r + 1, :].astype(F32), (8, HD)) for r in range(R)], 0)
        nv24 = jnp.concatenate([jnp.broadcast_to(nvv[r : r + 1, :].astype(F32), (8, HD)) for r in range(R)], 0)
        len24 = jnp.concatenate([jnp.full((8, 1), len_ref[r], jnp.int32) for r in range(R)], 0)
        scale = 1.0 / math.sqrt(HD)
        scores = jnp.concatenate([mm_t(q32, ckv[r])[r * 8 : (r + 1) * 8] for r in range(R)], 0) * scale
        self_score = jnp.sum(q24 * nk24, axis=1, keepdims=True) * scale
        live = iota((R * 8, SPAN), 1) < len24
        scores = jnp.where(live, scores, -1e30)
        highest = jnp.maximum(jnp.max(scores, axis=1, keepdims=True), self_score)
        expos = jnp.where(live, jnp.exp(scores - highest), 0.0)
        own_exp = jnp.exp(self_score - highest)
        totals = jnp.sum(expos, axis=1, keepdims=True) + own_exp
        weights = jnp.concatenate([expos / totals, jnp.zeros((8, SPAN), F32)], axis=0).astype(BF)
        own_weight = (own_exp / totals).astype(BF).astype(F32)
        summed = jnp.concatenate([mm(weights, cvv[r])[r * 8 : (r + 1) * 8] for r in range(R)], 0)
        summed = summed + own_weight * nv24
        at[pl.ds(pl.multiple_of((seat * 4 + y) * 32, 16), 32), :] = jnp.concatenate(
            [summed, jnp.zeros((8, HD), F32)], axis=0
        ).astype(BF)

    with jax.named_scope("entry"):
        pl.semaphore_wait(barrier, len(peers))

    sends = []
    def block_of(d):
        return rows(w2, (lax.rem(quad - d + 4, 4) * 2 + c) * 2 * KR, 2 * KR)

    o_cps = {d: send(block_of(0), block_of(0), osend.at[d], orecv.at[d], at_z(4 * d)) for d in (2, 1, 3)}
    c_cps = [send(block_of(0), block_of(0), csend.at[0], crecv.at[0], sibling)]
    mine = rows(at, (seat * 4 + y) * 32, 32)
    a_cps = [
        send(mine, mine, asend.at[k * 4 + m], arecv.at[k * 4 + m], in_quad(lax.rem(seat + k, 4), 0, m))
        for k, m in others
    ]
    w_cps = []
    for k, (src, dst, base) in enumerate(expert_weights):
        w_cps.append(send(src, rows(dst, base + c * F2, F2), wsend.at[k], wrecv.at[k], sibling))

    for cp in l_rest:
        cp.wait()
    row16, lane16 = iota((16, 4 * R), 0), iota((16, 4 * R), 1)
    part = row16 & 3
    wanted = (lane16 == x * R + part) & (part < R)
    res16 = jnp.zeros((16, QW), F32)
    for q in range(4):
        res16 = res16 + mm(onehot(wanted & ((row16 >> 2) == q)), resv[:, q * QW : (q + 1) * QW])
    gain_row = gainv[...].reshape(1, WD)
    gain16 = jnp.concatenate(
        [jnp.broadcast_to(gain_row[:, q * QW : (q + 1) * QW].astype(F32), (4, QW)) for q in range(4)], 0
    )
    gwf = gwv[...].astype(F32)
    expert = iota((128, 4 * R), 0)
    shares = jnp.zeros((128, 4 * R), F32)
    for k in range(4):
        shares = shares + jnp.where(expert == eidv[k : k + 1, :], gwf[k : k + 1, :], 0.0)
    share16 = mm_t(onehot(lane16 == x * R + (row16 >> 2)), shares.astype(BF))

    with jax.named_scope("attended_gather"):
        for cp in a_cps:
            cp.wait_recv()
        p, s = iota((HG * 64, 512), 0), iota((HG * 64, 512), 1)
        pick = onehot(s == ((p & 63) >> 2) * 32 + (p & 3) * 8 + (p >> 6))
        heads = mm(pick, at[...]).astype(BF)
        a64 = jnp.concatenate([heads[h * 64 : (h + 1) * 64] for h in range(HG)], axis=1)
        j = iota((1, 16 * KR), 1)
        slot = quotient(j, 2 * KR)
        rem = j - slot * 2 * KR
        later = rem >= KR
        source = (((slot >> 1) * 4 + seat) * 2 + (slot & 1)) * KR + jnp.where(later, rem - KR, rem)
        wide = mm(a64, onehot(iota((KG, 16 * KR), 0) == source))
        a2[...] = jnp.concatenate([jnp.where(later, 0.0, wide), jnp.where(later, wide, 0.0)], axis=0).astype(BF)

    with jax.named_scope("projection_gather"):
        for d in (1, 3, 2):
            o_cps[d].wait_recv()
            c_cps.append(send(block_of(d), block_of(d), csend.at[d], crecv.at[d], sibling))

    with jax.named_scope("gain_sums"):
        for cp in loads:
            cp.wait()
        for cp in w_cps:
            cp.wait_recv()
        gains = jnp.broadcast_to(gain_row, (16, WD))
        for lo, hi in ((0, 512), (512, 1024), (1024, 2 * FC)):
            gs[pl.ds(pl.multiple_of(y * 8, 8), 8), lo:hi] = mm_t(gains, wgu[lo:hi, :])[0:8]
        mine = gs.at[pl.ds(pl.multiple_of(y * 8, 8), 8)]
        g_cps = [send(mine, mine, tsend.at[d - 1], trecv.at[d - 1], at_y(d)) for d in range(1, NX)]

    with jax.named_scope("projection"):
        for cp in c_cps:
            cp.wait_recv()
        mixed = mm(a2[...], w2[...]).astype(BF)
        p, s = iota((256, 128), 0), iota((256, 128), 1)
        source = (((p >> 3) & 1) << 6) + ((p >> 4) << 2) + (p & 3)
        odd = ((p >> 2) & 1) == 1
        xs[...] = (
            mm(onehot((s == source) & ~odd), mixed[:, :QW]) + mm(onehot((s == source) & odd), mixed[:, QW:])
        ).astype(BF)

    with jax.named_scope("projection_terms"):
        slot = (seat * 4 + x) * 16
        cps = []
        for k, m in others:
            to = lax.rem(seat + k, 4)
            n = k * 4 + m
            cps.append(
                send(
                    rows(xs, (to * 4 + lax.rem(x + m, NX)) * 16, 16), rows(xr, slot, 16),
                    xsend.at[n], xrecv.at[n], in_quad(to, m, 0),
                )
            )
        for cp in cps:
            cp.wait_recv()
        sends += cps
        xr[pl.ds(pl.multiple_of(slot, 16), 16), :] = xs[pl.ds(pl.multiple_of(slot, 16), 16), :]
        hidden = res16
        for g in range(16):
            hidden = hidden + xr[g * 16 : (g + 1) * 16, :].astype(F32)
        hidden = hidden.astype(BF).astype(F32)

    with jax.named_scope("center_slice"):
        def per_request(v):
            v = jnp.sum(v, axis=1, keepdims=True)
            v = v[0:8] + v[8:16]
            v = v[0:4] + v[4:8]
            return jnp.concatenate([v] * 4, axis=0)

        def halves(v):
            high = v.astype(BF).astype(F32)
            return high, v - high

        mean = (per_request(hidden) / WD).astype(BF).astype(F32)
        inside = (iota((16, QW), 0) & 3) < R
        near = jnp.where(inside, hidden - mean, 0.0)
        notes = (mean,) + halves(per_request(near)) + halves(per_request(near * near))
        lane = iota((16, 128), 1)
        row = iota((16, 128), 0)
        extra = jnp.where(lane < 8, share16, 0.0)
        for j, note in enumerate(notes):
            by_request = jnp.concatenate([jnp.broadcast_to(note[i : i + 1], (4, 1)) for i in range(4)], axis=0)
            extra = extra + jnp.where(lane == 8 + j, by_request, 0.0)
        extra = jnp.where((row & 3) == R, extra, 0.0)
        extra = jnp.concatenate([extra, jnp.zeros((16, QW - 128), F32)], axis=1)
        hb[pl.ds(pl.multiple_of((x * NZ + z) * 16, 16), 16), :] = (near * gain16 + extra).astype(BF)

    with jax.named_scope("token_gather"):
        f_cps = []

        def over_x(d):
            blk = rows(hb, (x * NZ + lax.rem(z - d + NZ, NZ)) * 16, 16)
            for k in (2, 1, 3):
                n = (k - 1) * NZ + d % NZ
                f_cps.append(send(blk, blk, fsend.at[n], frecv.at[n], at_x(k)))

        blk = rows(hb, (x * NZ + z) * 16, 16)
        h_cps = {}
        for d in (4, -4, 3, -3, 2, -2, 1, -1):
            h_cps[d] = send(blk, blk, hsend.at[d % NZ], hrecv.at[d % NZ], at_z(d))
        over_x(0)
        for sign in (1, -1):
            h_cps[sign * 4].wait_recv()
            blk = rows(hb, (x * NZ + lax.rem(z - sign * 4 + NZ, NZ)) * 16, 16)
            for s in (4, 3, 2, 1) if sign > 0 else (3, 2, 1):
                n = sign * (4 + s)
                h_cps[n] = send(blk, blk, hsend.at[n % NZ], hrecv.at[n % NZ], at_z(sign * s))
        for d in (4, -4):
            over_x(d)
        for d in (1, -1, 2, -2, 3, -3, 5, -5, 6, -6, 7, -7, 8):
            h_cps[d].wait_recv()
            over_x(d)
        for cp in f_cps:
            cp.wait_recv()

    with jax.named_scope("compact"):
        p, s = iota((4 * ZR, NZ * 16), 0), iota((4 * ZR, NZ * 16), 1)
        quarter = quotient(p, ZR)
        m = p - quarter * ZR
        who = quotient(m, R)
        pick = onehot(s == who * 16 + quarter * 4 + (m - who * R))
        for g in range(NX):
            got = mm(pick, hb[g * NZ * 16 : (g + 1) * NZ * 16, :]).astype(BF)
            for q in range(4):
                nm[g * ZR : (g + 1) * ZR, q * QW : (q + 1) * QW] = got[q * ZR : (q + 1) * ZR]
        p, s = iota((ZR, NZ * 16), 0), iota((ZR, NZ * 16), 1)
        who = quotient(p, R)
        pick = onehot(s == who * 16 + (p - who * R) * 4 + R)
        for g in range(NX):
            gu[g * ZR : (g + 1) * ZR, 2 * FC : 2 * FC + 16] = mm(
                pick, hb[g * NZ * 16 : (g + 1) * NZ * 16, 0:128]
            )[:, 0:16].astype(BF)

    with jax.named_scope("gate_up"):
        tokens = nm[...]
        for lo, hi in ((0, 512), (512, 1024), (1024, 2 * FC)):
            gu[:, lo:hi] = mm_t(tokens, wgu[lo:hi, :]).astype(BF)

    with jax.named_scope("gate_up_terms"):
        cps = []
        for d in range(1, NX):
            to = lax.rem(y + d, NX)
            cps.append(send(rows(gu, to * ZR, ZR), rows(gr, y * ZR, ZR), gsend.at[d - 1], grecv.at[d - 1], at_y(d)))
        for cp in cps:
            cp.wait_recv()
        sends += cps + g_cps
        gr[pl.ds(pl.multiple_of(y * ZR, 16), ZR), :] = gu[pl.ds(pl.multiple_of(y * ZR, 16), ZR), :]

    with jax.named_scope("activation"):
        total = gr[0:ZR, :].astype(F32)
        for g in range(1, NX):
            total = total + gr[g * ZR : (g + 1) * ZR, :].astype(F32)
        for cp in g_cps:
            cp.wait_recv()
        notes = [gr[g * ZR : (g + 1) * ZR, 2 * FC : 2 * FC + 16].astype(F32) for g in range(NX)]
        means = [n[:, 8:9] for n in notes]
        sums = [n[:, 9:10] + n[:, 10:11] for n in notes]
        squares = [n[:, 11:12] + n[:, 12:13] for n in notes]
        center = sum(s + WD * m for s, m in zip(sums, means)) / D
        apart = [m - center for m in means]
        spread = sum(q + 2.0 * a * s + WD * a * a for q, a, s in zip(squares, apart, sums)) / D
        whole = total[:, : 2 * FC]
        for g in range(NX):
            whole = whole + apart[g] * gs[g * 8 : g * 8 + 1, :]
        whole = whole * lax.rsqrt(spread + EPS)
        lane = iota((ZR, 16), 1)
        share0 = jnp.sum(jnp.where(lane == x * 2, notes[0], 0.0), axis=1, keepdims=True)
        share1 = jnp.sum(jnp.where(lane == x * 2 + 1, notes[0], 0.0), axis=1, keepdims=True)
        gate, up = whole[:, :FC], whole[:, FC:]
        unit = iota((ZR, FC), 1)
        unit = jnp.where(unit >= F2, unit - F2, unit)
        share = jnp.where(unit >= F2 // 2, share1, share0)
        mine = rows(ac, y * ZR, ZR)
        ac[pl.ds(pl.multiple_of(y * ZR, 16), ZR), :] = (gate / (1.0 + jnp.exp(-gate)) * up * share).astype(BF)

    with jax.named_scope("activation_gather"):
        cps = [send(mine, mine, bsend.at[d - 1], brecv.at[d - 1], at_y(d)) for d in range(1, NX)]
        for cp in cps:
            cp.wait_recv()
        sends += cps

    with jax.named_scope("down"):
        act = ac[...]
        for t in range(3):
            n = WD // 3
            ms[:, t * n : (t + 1) * n] = mm(act, wdn[:, t * n : (t + 1) * n]).astype(BF)

    with jax.named_scope("expert_sum_x"):
        cps = []
        for d in range(1, NX):
            to = lax.rem(x + d, NX)
            cps.append(send(rows(ms, to * ZR, ZR), rows(mr, x * ZR, ZR), msend.at[d - 1], mrecv.at[d - 1], at_x(d)))
        for cp in cps:
            cp.wait_recv()
        sends += cps
        mr[pl.ds(pl.multiple_of(x * ZR, 16), ZR), :] = ms[pl.ds(pl.multiple_of(x * ZR, 16), ZR), :]
        total = mr[0:ZR, :].astype(F32)
        for g in range(1, NX):
            total = total + mr[g * ZR : (g + 1) * ZR, :].astype(F32)
        total = total.astype(BF)
        p, s = iota((NZ * 16, ZR), 0), iota((NZ * 16, ZR), 1)
        wanted = (s == (p >> 4) * R + (p & 3)) & ((p & 3) < R)
        piece = jnp.zeros((NZ * 16, QW), F32)
        for q in range(4):
            piece = piece + mm(onehot(wanted & (((p >> 2) & 3) == q)), total[:, q * QW : (q + 1) * QW])
        zs[...] = piece.astype(BF)

    with jax.named_scope("expert_sum_z"):
        cps = []
        for d in [8] + [v for i in range(7, 0, -1) for v in (i, NZ - i)]:
            to = lax.rem(z + d, NZ)
            cps.append(send(rows(zs, to * 16, 16), rows(zr, z * 16, 16), zsend.at[d], zrecv.at[d], at_z(d)))
        for cp in cps:
            cp.wait_recv()
        sends += cps
        zr[pl.ds(pl.multiple_of(z * 16, 16), 16), :] = zs[pl.ds(pl.multiple_of(z * 16, 16), 16), :]
        total = hidden
        for g in range(NZ):
            total = total + zr[g * 16 : (g + 1) * 16, :].astype(F32)
        for q in range(4):
            out_ref[:, q * QW : (q + 1) * QW] = total[q * 4 : q * 4 + R, :].astype(BF)

    with jax.named_scope("drain"):
        for cp in a_cps + list(o_cps.values()) + c_cps + w_cps + list(h_cps.values()) + f_cps + sends:
            cp.wait_send()


def on_device(
    queries, new_key, new_value, cache_keys, cache_values, lengths, out_proj, residual, norm_gain,
    expert_ids, gate_weights, gate_proj, up_proj, down_proj,
):
    vmem = pl.BlockSpec(memory_space=pltpu.VMEM)
    dma = pltpu.SemaphoreType.DMA
    return pl.pallas_call(
        kernel,
        out_shape=jax.ShapeDtypeStruct((R, WD), BF),
        in_specs=[pl.BlockSpec(memory_space=pltpu.SMEM)] + [pl.BlockSpec(memory_space=pl.ANY)] * 13,
        out_specs=vmem,
        scratch_shapes=[
            pltpu.VMEM((R, KG), BF),
            pltpu.VMEM((R, HD), BF),
            pltpu.VMEM((R, HD), BF),
            pltpu.VMEM((R, SPAN, HD), BF),
            pltpu.VMEM((R, SPAN, HD), BF),
            pltpu.VMEM((KR, WD), BF),
            pltpu.VMEM((4 * R, WD), BF),
            pltpu.VMEM((WD,), BF),
            pltpu.VMEM((4, 4 * R), jnp.int32),
            pltpu.VMEM((4, 4 * R), BF),
            pltpu.VMEM((2 * FC, WD), BF),
            pltpu.VMEM((FC, WD), BF),
            pltpu.VMEM((16 * KR, WD // 2), BF),
            pltpu.VMEM((16 * 32, HD), BF),
            pltpu.VMEM((128, 16 * KR), BF),
            pltpu.VMEM((256, QW), BF),
            pltpu.VMEM((256, QW), BF),
            pltpu.VMEM((NX * 8, 2 * FC), F32),
            pltpu.VMEM((NX * NZ * 16, QW), BF),
            pltpu.VMEM((ROWS, WD), BF),
            pltpu.VMEM((ROWS, GW), BF),
            pltpu.VMEM((ROWS, GW), BF),
            pltpu.VMEM((ROWS, FC), BF),
            pltpu.VMEM((ROWS, WD), BF),
            pltpu.VMEM((ROWS, WD), BF),
            pltpu.VMEM((NZ * 16, QW), BF),
            pltpu.VMEM((NZ * 16, QW), BF),
            dma((13,)),
            dma((3,)), dma((3,)),
            dma((4,)), dma((4,)),
            dma((4,)), dma((4,)),
            dma((16,)), dma((16,)),
            dma((16,)), dma((16,)),
            dma((3,)), dma((3,)),
            dma((NZ,)), dma((NZ,)),
            dma((3 * NZ,)), dma((3 * NZ,)),
            dma((3,)), dma((3,)),
            dma((3,)), dma((3,)),
            dma((3,)), dma((3,)),
            dma((NZ,)), dma((NZ,)),
        ],
        compiler_params=pltpu.CompilerParams(
            collective_id=0, has_side_effects=True, vmem_limit_bytes=62 << 20
        ),
        name="decode_layer",
    )(
        lengths, queries, new_key, new_value, cache_keys, cache_values,
        out_proj.reshape(KR, WD), residual, norm_gain, expert_ids.T, gate_weights.T,
        gate_proj.reshape(F2, WD), up_proj.reshape(F2, WD), down_proj.reshape(F2, WD),
    )


def solution(mesh):
    placed = (
        P(("attn", "eslice"), "egrp"),
        P(("attn", "eslice"), "egrp"),
        P(("attn", "eslice"), "egrp"),
        P(("attn", "eslice"), None, "egrp"),
        P(("attn", "eslice"), None, "egrp"),
        P(("attn", "eslice")),
        P("egrp", "attn", "eslice"),
        P("attn", "eslice"),
        P("eslice"),
        P("attn", None),
        P("attn", None),
        P("egrp", "attn", "eslice"),
        P("egrp", "attn", "eslice"),
        P("egrp", "attn", "eslice"),
    )
    return jax.shard_map(
        on_device, mesh=mesh, in_specs=placed, out_specs=P(("attn", "egrp"), "eslice"), check_vma=False
    )
```

time: 121 us -> 95 us (0.79)
  the two profiles are of different devices: /device:TPU:1 before, /device:TPU:32 now
where the time goes in v2:
time: 95 us; the launch traced here: 94.8 us
  Pallas kernels  93.5 us (98%)
  local copies, waits for them, and re-layouts  1.31 us (1%)
    pallas_call x1, Pallas kernels, on_device(): pl.pallas_call(kernel, out_shape=jax.ShapeDtypeStruct((R, WD), BF), in_sp...  93.5 us

profile of v2, /device:TPU:32, one launch (start us, length us, event | category | flops | bytes accessed | tf_op | source)
XLA Modules:
  0.0 94.8 jit_solution(568903218309675132)
XLA Ops:
  0.0 93.5 %decode_layer.1 = bf16[3,1536]{1,0:T(4,128)(2,1)} custom-call(s32[3]{0:T(128)} %len_ref.1, bf16[3,768]{1,0:T(4,128)(2,1)} %q_hbm.1, bf16[3,128]{1,0:T(4,128)(2,1)} %nk_hbm.1, bf16[3,128]{1,0:T(4,128)(2,1)} %nv_hbm.1, bf16[3,512,128]{2,1,0:T(8,128)(2,1)} %ck_hbm.1, bf16[3,512,128]{2,1,0:T(8,128)(2,1)} %cv_hbm.1, bf16[24,1536]{1,0:T(8,128)(2,1)} %bitcast.9, ...), custom_call_target="tpu_custom_call" | custom-call | tf_op jit(solution)/shard_map/decode_layer/pallas_call | solution.py:427
  93.5 1.3 %copy.16 = bf16[3,1536]{1,0:T(4,128)(2,1)} copy(bf16[3,1536]{1,0:T(4,128)(2,1)} %decode_layer.1) | data formatting | bytes 18432

commit v3 on v2

--- a/solution.py
+++ b/solution.py
@@ -22,6 +22,7 @@
 F2 = 336
 FC = 2 * F2
 ZR = NZ * R
+NT, WT = 1, WD
 GW = 2 * FC + 64
 ROWS = NX * ZR
 MESH = pl.DeviceIdType.MESH
@@ -53,7 +54,7 @@
     len_ref, q_hbm, nk_hbm, nv_hbm, ck_hbm, cv_hbm, op_hbm, res_hbm, gain_hbm, eid_hbm, gw_hbm,
     wg_ref, wu_ref, wd_ref,
     out_ref,
-    qv, nkv, nvv, ckv, cvv, opv, resv, gainv, eidv, gwv, wgu, wdn, w2, at, a2, xs, xr, gs, hb, nm, gu, gr, ac, ms, mr, zs, zr,
+    qv, nkv, nvv, ckv, cvv, opv, resv, gainv, eidv, gwv, wgu, wdn, w2, at, a2, xs, xr, gs, hb, nm, gu, gr, ac, ms, mr, zs, zl, zc, zr,
     load_sem, wsend, wrecv, osend, orecv, csend, crecv, asend, arecv, xsend, xrecv, tsend, trecv,
     hsend, hrecv, fsend, frecv, gsend, grecv, bsend, brecv, msend, mrecv, zsend, zrecv,
 ):
@@ -78,7 +79,7 @@
     sibling = (z * 2 + 1 - c, x, y)
     others = [(k // 4, k % 4) for k in range(1, 16)]
     peers = [sibling]
-    peers += [at_z(d) for d in range(1, NZ)]
+    peers += [at_z(d) for d in range(-4, 5) if d]
     peers += [at_x(d) for d in range(1, NX)] + [at_y(d) for d in range(1, NX)]
     peers += [in_quad(lax.rem(seat + k, 4), m, 0) for k, m in others if k and m]
     peers += [in_quad(lax.rem(seat + k, 4), 0, m) for k, m in others if k and m]
@@ -122,6 +123,22 @@
     own = opv[...].astype(F32)
     block = jnp.concatenate([own[:, : WD // 2], own[:, WD // 2 :]], axis=0).astype(BF)
     w2[pl.ds(pl.multiple_of((quad * 2 + c) * 2 * KR, 16), 2 * KR), :] = block
+
+    sends = []
+    with jax.named_scope("entry"):
+        pl.semaphore_wait(barrier, len(peers))
+
+    def block_of(d):
+        return rows(w2, (lax.rem(quad - d + 8, 4) * 2 + c) * 2 * KR, 2 * KR)
+
+    def pass_block(d, half, k, to):
+        part = w2.at[
+            pl.ds(pl.multiple_of((lax.rem(quad - d + 8, 4) * 2 + c) * 2 * KR, 16), 2 * KR), half * QW : (half + 1) * QW
+        ]
+        return send(part, part, osend.at[k], orecv.at[k], at_z(to))
+
+    o_cps = [pass_block(0, 0, 0, 4), pass_block(0, 1, 1, -4), pass_block(0, 1, 2, 4), pass_block(0, 0, 3, -4)]
+    c_cps = [send(block_of(0), block_of(0), csend.at[0], crecv.at[0], sibling)]
 
     with jax.named_scope("attention"):
         for cp in (l_q, l_nk, l_nv, l_ck, l_cv):
@@ -153,15 +170,6 @@
             [summed, jnp.zeros((8, HD), F32)], axis=0
         ).astype(BF)
 
-    with jax.named_scope("entry"):
-        pl.semaphore_wait(barrier, len(peers))
-
-    sends = []
-    def block_of(d):
-        return rows(w2, (lax.rem(quad - d + 4, 4) * 2 + c) * 2 * KR, 2 * KR)
-
-    o_cps = {d: send(block_of(0), block_of(0), osend.at[d], orecv.at[d], at_z(4 * d)) for d in (2, 1, 3)}
-    c_cps = [send(block_of(0), block_of(0), csend.at[0], crecv.at[0], sibling)]
     mine = rows(at, (seat * 4 + y) * 32, 32)
     a_cps = [
         send(mine, mine, asend.at[k * 4 + m], arecv.at[k * 4 + m], in_quad(lax.rem(seat + k, 4), 0, m))
@@ -190,6 +198,12 @@
         shares = shares + jnp.where(expert == eidv[k : k + 1, :], gwf[k : k + 1, :], 0.0)
     share16 = mm_t(onehot(lane16 == x * R + (row16 >> 2)), shares.astype(BF))
 
+    with jax.named_scope("projection_relay"):
+        o_cps[0].wait_recv()
+        o_cps.append(pass_block(1, 0, 4, 4))
+        o_cps[1].wait_recv()
+        o_cps.append(pass_block(-1, 1, 5, -4))
+
     with jax.named_scope("attended_gather"):
         for cp in a_cps:
             cp.wait_recv()
@@ -206,9 +220,11 @@
         a2[...] = jnp.concatenate([jnp.where(later, 0.0, wide), jnp.where(later, wide, 0.0)], axis=0).astype(BF)
 
     with jax.named_scope("projection_gather"):
-        for d in (1, 3, 2):
-            o_cps[d].wait_recv()
-            c_cps.append(send(block_of(d), block_of(d), csend.at[d], crecv.at[d], sibling))
+        for d, first, second in ((1, 0, 2), (-1, 1, 3), (2, 4, 5)):
+            if d == 2:
+                o_cps[first].wait_recv()
+            o_cps[second].wait_recv()
+            c_cps.append(send(block_of(d), block_of(d), csend.at[d % 4], crecv.at[d % 4], sibling))
 
     with jax.named_scope("gain_sums"):
         for cp in loads:
@@ -374,47 +390,79 @@
 
     with jax.named_scope("down"):
         act = ac[...]
-        for t in range(3):
-            n = WD // 3
-            ms[:, t * n : (t + 1) * n] = mm(act, wdn[:, t * n : (t + 1) * n]).astype(BF)
-
-    with jax.named_scope("expert_sum_x"):
-        cps = []
-        for d in range(1, NX):
-            to = lax.rem(x + d, NX)
-            cps.append(send(rows(ms, to * ZR, ZR), rows(mr, x * ZR, ZR), msend.at[d - 1], mrecv.at[d - 1], at_x(d)))
-        for cp in cps:
-            cp.wait_recv()
-        sends += cps
-        mr[pl.ds(pl.multiple_of(x * ZR, 16), ZR), :] = ms[pl.ds(pl.multiple_of(x * ZR, 16), ZR), :]
-        total = mr[0:ZR, :].astype(F32)
+        m_cps = []
+        for t in range(NT):
+            cols = slice(t * WT, (t + 1) * WT)
+            for lo in range(0, WT, 512):
+                ms[:, lo : lo + 512] = mm(act, wdn[:, lo : lo + 512]).astype(BF)
+            for d in range(1, NX):
+                to = lax.rem(x + d, NX)
+                n = t * 3 + d - 1
+                m_cps.append(
+                    send(
+                        ms.at[pl.ds(pl.multiple_of(to * ZR, 16), ZR), cols],
+                        mr.at[pl.ds(pl.multiple_of(x * ZR, 16), ZR), cols],
+                        msend.at[n], mrecv.at[n], at_x(d),
+                    )
+                )
+
+    p, s = iota((NZ * 16, ZR), 0), iota((NZ * 16, ZR), 1)
+    wanted = (s == (p >> 4) * R + (p & 3)) & ((p & 3) < R)
+    picks = [onehot(wanted & (((p >> 2) & 3) == q)) for q in range(4)]
+    z_cps = {}
+
+    def piece(t, d):
+        return pl.ds(pl.multiple_of(t * NZ * 16 + lax.rem(z + d + NZ, NZ) * 16, 16), 16)
+
+    def slot(t, n, k):
+        return slice((t * n + k) * 16, (t * n + k + 1) * 16)
+
+    def sum_over_x(t):
+        cols = slice(t * WT, (t + 1) * WT)
+        for cp in m_cps[t * 3 : t * 3 + 3]:
+            cp.wait_recv()
+        here = pl.ds(pl.multiple_of(x * ZR, 16), ZR)
+        mr[here, cols] = ms[here, cols]
+        total = mr[0:ZR, cols].astype(F32)
         for g in range(1, NX):
-            total = total + mr[g * ZR : (g + 1) * ZR, :].astype(F32)
+            total = total + mr[g * ZR : (g + 1) * ZR, cols].astype(F32)
         total = total.astype(BF)
-        p, s = iota((NZ * 16, ZR), 0), iota((NZ * 16, ZR), 1)
-        wanted = (s == (p >> 4) * R + (p & 3)) & ((p & 3) < R)
-        piece = jnp.zeros((NZ * 16, QW), F32)
+        tiles = jnp.zeros((NZ * 16, WT // 4), F32)
         for q in range(4):
-            piece = piece + mm(onehot(wanted & (((p >> 2) & 3) == q)), total[:, q * QW : (q + 1) * QW])
-        zs[...] = piece.astype(BF)
-
-    with jax.named_scope("expert_sum_z"):
-        cps = []
-        for d in [8] + [v for i in range(7, 0, -1) for v in (i, NZ - i)]:
-            to = lax.rem(z + d, NZ)
-            cps.append(send(rows(zs, to * 16, 16), rows(zr, z * 16, 16), zsend.at[d], zrecv.at[d], at_z(d)))
-        for cp in cps:
-            cp.wait_recv()
-        sends += cps
-        zr[pl.ds(pl.multiple_of(z * 16, 16), 16), :] = zs[pl.ds(pl.multiple_of(z * 16, 16), 16), :]
-        total = hidden
-        for g in range(NZ):
-            total = total + zr[g * 16 : (g + 1) * 16, :].astype(F32)
-        for q in range(4):
-            out_ref[:, q * QW : (q + 1) * QW] = total[q * 4 : q * 4 + R, :].astype(BF)
+            tiles = tiles + mm(picks[q], total[:, q * WT // 4 : (q + 1) * WT // 4])
+        zs[t * NZ * 16 : (t + 1) * NZ * 16, :] = tiles.astype(BF)
+        for k, d in ((3, 8), (2, 7), (6, -7), (1, 6), (5, -6), (0, 5), (4, -5)):
+            to = d - 4 if d > 0 else d + 4
+            n = t * 15 + k
+            z_cps[n] = send(zs.at[piece(t, d)], zl.at[slot(t, 7, k)], zsend.at[n], zrecv.at[n], at_z(to))
+        for k, d in ((2, 3), (5, -3), (1, 2), (4, -2), (0, 1), (3, -1)):
+            n = t * 15 + 7 + k
+            z_cps[n] = send(zs.at[piece(t, d)], zr.at[slot(t, 8, k)], zsend.at[n], zrecv.at[n], at_z(d))
+
+    def relay(t):
+        for way, d, ks in ((0, 4, (0, 1, 2, 3)), (1, -4, (4, 5, 6))):
+            total = zs[piece(t, d), :].astype(F32)
+            for k in ks:
+                z_cps[t * 15 + k].wait_recv()
+                total = total + zl[slot(t, 7, k), :].astype(F32)
+            zc[slot(t, 2, way), :] = total.astype(BF)
+            n = t * 15 + 13 + way
+            z_cps[n] = send(zc.at[slot(t, 2, way)], zr.at[slot(t, 8, 6 + way)], zsend.at[n], zrecv.at[n], at_z(d))
+
+    with jax.named_scope("expert_sums"):
+        sum_over_x(0)
+        relay(0)
+    with jax.named_scope("last_sum"):
+        for t in range(NT):
+            total = zs[piece(t, 0), :].astype(F32)
+            for k in range(8):
+                z_cps[t * 15 + 7 + k].wait_recv()
+                total = total + zr[slot(t, 8, k), :].astype(F32)
+            for q in range(4):
+                out_ref[:, q * QW : (q + 1) * QW] = (hidden + total)[q * 4 : q * 4 + R].astype(BF)
 
     with jax.named_scope("drain"):
-        for cp in a_cps + list(o_cps.values()) + c_cps + w_cps + list(h_cps.values()) + f_cps + sends:
+        for cp in a_cps + o_cps + c_cps + w_cps + m_cps + list(z_cps.values()) + list(h_cps.values()) + f_cps + sends:
             cp.wait_send()
 
 
@@ -455,11 +503,13 @@
             pltpu.VMEM((ROWS, FC), BF),
             pltpu.VMEM((ROWS, WD), BF),
             pltpu.VMEM((ROWS, WD), BF),
-            pltpu.VMEM((NZ * 16, QW), BF),
-            pltpu.VMEM((NZ * 16, QW), BF),
+            pltpu.VMEM((NT * NZ * 16, WT // 4), BF),
+            pltpu.VMEM((NT * 7 * 16, WT // 4), BF),
+            pltpu.VMEM((NT * 2 * 16, WT // 4), BF),
+            pltpu.VMEM((NT * 8 * 16, WT // 4), BF),
             dma((13,)),
             dma((3,)), dma((3,)),
-            dma((4,)), dma((4,)),
+            dma((6,)), dma((6,)),
             dma((4,)), dma((4,)),
             dma((16,)), dma((16,)),
             dma((16,)), dma((16,)),
@@ -468,8 +518,8 @@
             dma((3 * NZ,)), dma((3 * NZ,)),
             dma((3,)), dma((3,)),
             dma((3,)), dma((3,)),
-            dma((3,)), dma((3,)),
-            dma((NZ,)), dma((NZ,)),
+            dma((3 * NT,)), dma((3 * NT,)),
+            dma((15 * NT,)), dma((15 * NT,)),
         ],
         compiler_params=pltpu.CompilerParams(
             collective_id=0, has_side_effects=True, vmem_limit_bytes=62 << 20

time: 95 us -> 91.6 us (0.964)
  Pallas kernels: 93.5 us -> 90.1 us
    pallas_call x1, Pallas kernels: 93.5 us -> 90.1 us  [on_device(): pl.pallas_call(kernel, out_shape=jax.ShapeDtypeStruct((R, WD), BF), in_sp...]
where the time goes in v3:
time: 91.6 us; the launch traced here: 91.4 us
  Pallas kernels  90.1 us (98%)
  local copies, waits for them, and re-layouts  1.31 us (1%)
    pallas_call x1, Pallas kernels, on_device(): pl.pallas_call(kernel, out_shape=jax.ShapeDtypeStruct((R, WD), BF), in_sp...  90.1 us

profile of v3, /device:TPU:32, one launch (start us, length us, event | category | flops | bytes accessed | tf_op | source)
XLA Modules:
  0.0 91.4 jit_solution(13815159677630180576)
XLA Ops:
  0.0 90.1 %decode_layer.1 = bf16[3,1536]{1,0:T(4,128)(2,1)} custom-call(s32[3]{0:T(128)} %len_ref.1, bf16[3,768]{1,0:T(4,128)(2,1)} %q_hbm.1, bf16[3,128]{1,0:T(4,128)(2,1)} %nk_hbm.1, bf16[3,128]{1,0:T(4,128)(2,1)} %nv_hbm.1, bf16[3,512,128]{2,1,0:T(8,128)(2,1)} %ck_hbm.1, bf16[3,512,128]{2,1,0:T(8,128)(2,1)} %cv_hbm.1, bf16[24,1536]{1,0:T(8,128)(2,1)} %bitcast.9, ...), custom_call_target="tpu_custom_call" | custom-call | tf_op jit(solution)/shard_map/decode_layer/pallas_call | solution.py:475
  90.1 1.3 %copy.16 = bf16[3,1536]{1,0:T(4,128)(2,1)} copy(bf16[3,1536]{1,0:T(4,128)(2,1)} %decode_layer.1) | data formatting | bytes 18432

commit v4 on v3

--- a/solution.py
+++ b/solution.py
@@ -23,7 +23,7 @@
 FC = 2 * F2
 ZR = NZ * R
 NT, WT = 1, WD
-GW = 2 * FC + 64
+GW = 768
 ROWS = NX * ZR
 MESH = pl.DeviceIdType.MESH
 BF = jnp.bfloat16
@@ -113,9 +113,9 @@
         load(src, dst, load_sem.at[k + 6])
         for k, (src, dst) in enumerate(((res_hbm, resv), (gain_hbm, gainv), (eid_hbm, eidv), (gw_hbm, gwv)))
     ]
-    expert_weights = ((wg_ref, wgu, 0), (wu_ref, wgu, FC), (wd_ref, wdn, 0))
+    expert_weights = ((wg_ref, wgu, c * FC), (wu_ref, wgu, c * FC + F2), (wd_ref, wdn, c * F2))
     loads = [
-        load(src, rows(dst, base + c * F2, F2), load_sem.at[k + 10])
+        load(src, rows(dst, base, F2), load_sem.at[k + 10])
         for k, (src, dst, base) in enumerate(expert_weights)
     ]
 
@@ -177,7 +177,7 @@
     ]
     w_cps = []
     for k, (src, dst, base) in enumerate(expert_weights):
-        w_cps.append(send(src, rows(dst, base + c * F2, F2), wsend.at[k], wrecv.at[k], sibling))
+        w_cps.append(send(src, rows(dst, base, F2), wsend.at[k], wrecv.at[k], sibling))
 
     for cp in l_rest:
         cp.wait()
@@ -336,65 +336,74 @@
         who = quotient(p, R)
         pick = onehot(s == who * 16 + (p - who * R) * 4 + R)
         for g in range(NX):
-            gu[g * ZR : (g + 1) * ZR, 2 * FC : 2 * FC + 16] = mm(
+            gu[g * ZR : (g + 1) * ZR, FC : FC + 16] = mm(
                 pick, hb[g * NZ * 16 : (g + 1) * NZ * 16, 0:128]
             )[:, 0:16].astype(BF)
 
     with jax.named_scope("gate_up"):
         tokens = nm[...]
-        for lo, hi in ((0, 512), (512, 1024), (1024, 2 * FC)):
-            gu[:, lo:hi] = mm_t(tokens, wgu[lo:hi, :]).astype(BF)
-
-    with jax.named_scope("gate_up_terms"):
-        cps = []
-        for d in range(1, NX):
-            to = lax.rem(y + d, NX)
-            cps.append(send(rows(gu, to * ZR, ZR), rows(gr, y * ZR, ZR), gsend.at[d - 1], grecv.at[d - 1], at_y(d)))
-        for cp in cps:
-            cp.wait_recv()
-        sends += cps + g_cps
-        gr[pl.ds(pl.multiple_of(y * ZR, 16), ZR), :] = gu[pl.ds(pl.multiple_of(y * ZR, 16), ZR), :]
+        y_cps = []
+        for h in range(2):
+            for lo, hi in ((0, 512), (512, FC)):
+                gu[h * ROWS : (h + 1) * ROWS, lo:hi] = mm_t(tokens, wgu[h * FC + lo : h * FC + hi, :]).astype(BF)
+            for d in range(1, NX):
+                to = lax.rem(y + d, NX)
+                n = h * 3 + d - 1
+                y_cps.append(
+                    send(
+                        rows(gu, h * ROWS + to * ZR, ZR), rows(gr, h * ROWS + y * ZR, ZR),
+                        gsend.at[n], grecv.at[n], at_y(d),
+                    )
+                )
 
     with jax.named_scope("activation"):
-        total = gr[0:ZR, :].astype(F32)
-        for g in range(1, NX):
-            total = total + gr[g * ZR : (g + 1) * ZR, :].astype(F32)
-        for cp in g_cps:
-            cp.wait_recv()
-        notes = [gr[g * ZR : (g + 1) * ZR, 2 * FC : 2 * FC + 16].astype(F32) for g in range(NX)]
-        means = [n[:, 8:9] for n in notes]
-        sums = [n[:, 9:10] + n[:, 10:11] for n in notes]
-        squares = [n[:, 11:12] + n[:, 12:13] for n in notes]
-        center = sum(s + WD * m for s, m in zip(sums, means)) / D
-        apart = [m - center for m in means]
-        spread = sum(q + 2.0 * a * s + WD * a * a for q, a, s in zip(squares, apart, sums)) / D
-        whole = total[:, : 2 * FC]
-        for g in range(NX):
-            whole = whole + apart[g] * gs[g * 8 : g * 8 + 1, :]
-        whole = whole * lax.rsqrt(spread + EPS)
-        lane = iota((ZR, 16), 1)
-        share0 = jnp.sum(jnp.where(lane == x * 2, notes[0], 0.0), axis=1, keepdims=True)
-        share1 = jnp.sum(jnp.where(lane == x * 2 + 1, notes[0], 0.0), axis=1, keepdims=True)
-        gate, up = whole[:, :FC], whole[:, FC:]
-        unit = iota((ZR, FC), 1)
-        unit = jnp.where(unit >= F2, unit - F2, unit)
-        share = jnp.where(unit >= F2 // 2, share1, share0)
-        mine = rows(ac, y * ZR, ZR)
-        ac[pl.ds(pl.multiple_of(y * ZR, 16), ZR), :] = (gate / (1.0 + jnp.exp(-gate)) * up * share).astype(BF)
+        b_cps = []
+        for h in range(2):
+            for cp in y_cps[h * 3 : h * 3 + 3]:
+                cp.wait_recv()
+            here = pl.ds(pl.multiple_of(h * ROWS + y * ZR, 16), ZR)
+            gr[here, :] = gu[here, :]
+            terms = [gr[h * ROWS + g * ZR : h * ROWS + (g + 1) * ZR, :].astype(F32) for g in range(NX)]
+            if h == 0:
+                for cp in g_cps:
+                    cp.wait_recv()
+                notes = [v[:, FC : FC + 16] for v in terms]
+                means = [n[:, 8:9] for n in notes]
+                sums = [n[:, 9:10] + n[:, 10:11] for n in notes]
+                squares = [n[:, 11:12] + n[:, 12:13] for n in notes]
+                center = sum(v + WD * m for v, m in zip(sums, means)) / D
+                apart = [m - center for m in means]
+                spread = sum(q + 2.0 * a * v + WD * a * a for q, a, v in zip(squares, apart, sums)) / D
+                norm = lax.rsqrt(spread + EPS)
+                lane = iota((ZR, 16), 1)
+                share0 = jnp.sum(jnp.where(lane == x * 2, notes[0], 0.0), axis=1, keepdims=True)
+                share1 = jnp.sum(jnp.where(lane == x * 2 + 1, notes[0], 0.0), axis=1, keepdims=True)
+                share = jnp.where(iota((ZR, F2), 1) >= F2 // 2, share1, share0)
+            whole = (terms[0] + terms[1])[:, :FC] + (terms[2] + terms[3])[:, :FC]
+            for g in range(NX):
+                whole = whole + apart[g] * gs[g * 8 : g * 8 + 1, :][:, h * FC : (h + 1) * FC]
+            whole = whole * norm
+            gate, up = whole[:, :F2], whole[:, F2:]
+            ac[here, 0:F2] = (gate / (1.0 + jnp.exp(-gate)) * up * share).astype(BF)
+            mine = rows(ac, h * ROWS + y * ZR, ZR)
+            for d in range(1, NX):
+                n = h * 3 + d - 1
+                b_cps.append(send(mine, mine, bsend.at[n], brecv.at[n], at_y(d)))
 
     with jax.named_scope("activation_gather"):
-        cps = [send(mine, mine, bsend.at[d - 1], brecv.at[d - 1], at_y(d)) for d in range(1, NX)]
-        for cp in cps:
-            cp.wait_recv()
-        sends += cps
+        for cp in b_cps:
+            cp.wait_recv()
+        sends += y_cps + b_cps + g_cps
 
     with jax.named_scope("down"):
-        act = ac[...]
+        act = [ac[h * ROWS : (h + 1) * ROWS, 0:F2] for h in range(2)]
         m_cps = []
         for t in range(NT):
             cols = slice(t * WT, (t + 1) * WT)
             for lo in range(0, WT, 512):
-                ms[:, lo : lo + 512] = mm(act, wdn[:, lo : lo + 512]).astype(BF)
+                ms[:, lo : lo + 512] = sum(
+                    mm(act[h], wdn[h * F2 : (h + 1) * F2, lo : lo + 512]) for h in range(2)
+                ).astype(BF)
             for d in range(1, NX):
                 to = lax.rem(x + d, NX)
                 n = t * 3 + d - 1
@@ -498,9 +507,9 @@
             pltpu.VMEM((NX * 8, 2 * FC), F32),
             pltpu.VMEM((NX * NZ * 16, QW), BF),
             pltpu.VMEM((ROWS, WD), BF),
-            pltpu.VMEM((ROWS, GW), BF),
-            pltpu.VMEM((ROWS, GW), BF),
-            pltpu.VMEM((ROWS, FC), BF),
+            pltpu.VMEM((2 * ROWS, GW), BF),
+            pltpu.VMEM((2 * ROWS, GW), BF),
+            pltpu.VMEM((2 * ROWS, 384), BF),
             pltpu.VMEM((ROWS, WD), BF),
             pltpu.VMEM((ROWS, WD), BF),
             pltpu.VMEM((NT * NZ * 16, WT // 4), BF),
@@ -516,8 +525,8 @@
             dma((3,)), dma((3,)),
             dma((NZ,)), dma((NZ,)),
             dma((3 * NZ,)), dma((3 * NZ,)),
-            dma((3,)), dma((3,)),
-            dma((3,)), dma((3,)),
+            dma((6,)), dma((6,)),
+            dma((6,)), dma((6,)),
             dma((3 * NT,)), dma((3 * NT,)),
             dma((15 * NT,)), dma((15 * NT,)),
         ],

time: 91.6 us -> 90.3 us (0.986)
  the two profiles are of different devices: /device:TPU:32 before, /device:TPU:16 now
where the time goes in v4:
time: 90.3 us; the launch traced here: 90.1 us
  Pallas kernels  88.7 us (98%)
  local copies, waits for them, and re-layouts  1.31 us (1%)
    pallas_call x1, Pallas kernels, on_device(): pl.pallas_call(kernel, out_shape=jax.ShapeDtypeStruct((R, WD), BF), in_sp...  88.7 us

profile of v4, /device:TPU:16, one launch (start us, length us, event | category | flops | bytes accessed | tf_op | source)
XLA Modules:
  0.0 90.1 jit_solution(7492878839287778969)
XLA Ops:
  0.0 88.7 %decode_layer.1 = bf16[3,1536]{1,0:T(4,128)(2,1)} custom-call(s32[3]{0:T(128)} %len_ref.1, bf16[3,768]{1,0:T(4,128)(2,1)} %q_hbm.1, bf16[3,128]{1,0:T(4,128)(2,1)} %nk_hbm.1, bf16[3,128]{1,0:T(4,128)(2,1)} %nv_hbm.1, bf16[3,512,128]{2,1,0:T(8,128)(2,1)} %ck_hbm.1, bf16[3,512,128]{2,1,0:T(8,128)(2,1)} %cv_hbm.1, bf16[24,1536]{1,0:T(8,128)(2,1)} %bitcast.9, ...), custom_call_target="tpu_custom_call" | custom-call | tf_op jit(solution)/shard_map/decode_layer/pallas_call | solution.py:484
  88.8 1.3 %copy.16 = bf16[3,1536]{1,0:T(4,128)(2,1)} copy(bf16[3,1536]{1,0:T(4,128)(2,1)} %decode_layer.1) | data formatting | bytes 18432

commit v5 on v4

--- a/solution.py
+++ b/solution.py
@@ -220,10 +220,8 @@
         a2[...] = jnp.concatenate([jnp.where(later, 0.0, wide), jnp.where(later, wide, 0.0)], axis=0).astype(BF)
 
     with jax.named_scope("projection_gather"):
-        for d, first, second in ((1, 0, 2), (-1, 1, 3), (2, 4, 5)):
-            if d == 2:
-                o_cps[first].wait_recv()
-            o_cps[second].wait_recv()
+        for d, k in ((1, 2), (-1, 3)):
+            o_cps[k].wait_recv()
             c_cps.append(send(block_of(d), block_of(d), csend.at[d % 4], crecv.at[d % 4], sibling))
 
     with jax.named_scope("gain_sums"):
@@ -236,6 +234,11 @@
             gs[pl.ds(pl.multiple_of(y * 8, 8), 8), lo:hi] = mm_t(gains, wgu[lo:hi, :])[0:8]
         mine = gs.at[pl.ds(pl.multiple_of(y * 8, 8), 8)]
         g_cps = [send(mine, mine, tsend.at[d - 1], trecv.at[d - 1], at_y(d)) for d in range(1, NX)]
+
+    with jax.named_scope("last_block"):
+        o_cps[4].wait_recv()
+        o_cps[5].wait_recv()
+        c_cps.append(send(block_of(2), block_of(2), csend.at[2], crecv.at[2], sibling))
 
     with jax.named_scope("projection"):
         for cp in c_cps:

time: 90.3 us -> 91.9 us (1.018)
  the two profiles are of different devices: /device:TPU:16 before, /device:TPU:32 now
where the time goes in v5:
time: 91.9 us; the launch traced here: 91.7 us
  Pallas kernels  90.4 us (98%)
  local copies, waits for them, and re-layouts  1.31 us (1%)
    pallas_call x1, Pallas kernels, on_device(): pl.pallas_call(kernel, out_shape=jax.ShapeDtypeStruct((R, WD), BF), in_sp...  90.4 us

profile of v5, /device:TPU:32, one launch (start us, length us, event | category | flops | bytes accessed | tf_op | source)
XLA Modules:
  0.0 91.7 jit_solution(17857490537087391526)
XLA Ops:
  0.0 90.4 %decode_layer.1 = bf16[3,1536]{1,0:T(4,128)(2,1)} custom-call(s32[3]{0:T(128)} %len_ref.1, bf16[3,768]{1,0:T(4,128)(2,1)} %q_hbm.1, bf16[3,128]{1,0:T(4,128)(2,1)} %nk_hbm.1, bf16[3,128]{1,0:T(4,128)(2,1)} %nv_hbm.1, bf16[3,512,128]{2,1,0:T(8,128)(2,1)} %ck_hbm.1, bf16[3,512,128]{2,1,0:T(8,128)(2,1)} %cv_hbm.1, bf16[24,1536]{1,0:T(8,128)(2,1)} %bitcast.9, ...), custom_call_target="tpu_custom_call" | custom-call | tf_op jit(solution)/shard_map/decode_layer/pallas_call | solution.py:487
  90.4 1.3 %copy.16 = bf16[3,1536]{1,0:T(4,128)(2,1)} copy(bf16[3,1536]{1,0:T(4,128)(2,1)} %decode_layer.1) | data formatting | bytes 18432
